TPU v7x, 32 devices: a whole 2x2x4 slice. The times are simulated.
32 devices in a mesh: seq: 4 (over y, x), tp: 8 (over z, core).
Axes of the slice: x: 2, y: 2, z: 4, core: 2. Of those that a mesh axis runs over, the one named last changes fastest.
Arguments:
- projected: bfloat16 [3, 4096, 8192], P(None, 'seq', 'tp'), may hold values from -6 to 6
- short_filter: float32 [3, 3, 8192], P(None, None, 'tp'), may hold values from -2.5 to 2.5
- residue: float32 [512, 16], P('tp'), may hold values from -1.5 to 1.5
- rate: float32 [512, 16], P('tp'), may hold values from 0 to 1, as said below
- out_weight: bfloat16 [8192, 8192], P('tp'), may hold values from -0.0625 to 0.0625
Outputs:
- output: bfloat16 [4096, 8192], P(('seq', 'tp'))
Inputs may be any that keep to these rules, and one draw needn't show every extreme that they name: Every rate is positive.
All inputs are finite; a program needn't handle non-finite values.
Results may differ from a plain program's by a relative error of at most 0.02.
Values may be sent and summed in bfloat16 or wider, within the bound.
A program may use at most 128 MiB of HBM per device.

v0:
```python
import jax
import jax.numpy as jnp
from jax import lax
from jax.sharding import PartitionSpec as P

GROUP = 16
MODES = 16


def passed_along(value, axis, steps):
    count = lax.axis_size(axis)
    leading, last = (max(0, -steps), min(count, count - steps))
    return lax.ppermute(value, axis, [(source, source + steps) for source in range(leading, last)])


def toeplitz_from(kernel, block_len):
    group_count = kernel.shape[0]
    padded = jnp.concatenate(
        [
            jnp.zeros((group_count, block_len - 1), jnp.float32),
            kernel,
            jnp.zeros((group_count, 1), jnp.float32),
        ],
        axis=1,
    )
    tiled = jnp.tile(padded, (1, block_len))
    width = 2 * block_len - 1
    trimmed = tiled[:, : block_len * width].reshape(group_count, block_len, width)
    hankel = trimmed[:, :, block_len - 1 : width]
    return jnp.swapaxes(hankel, 1, 2)


def filter_tables(rate, residue, block_len):
    mode_weight = residue * jnp.sqrt(-jnp.expm1(-2.0 * rate))
    offsets = lax.iota(jnp.int32, block_len)
    lag_float = offsets.astype(jnp.float32)
    powers = jnp.exp(-rate[None, :, :] * lag_float[:, None, None])
    kernel = jnp.einsum("tgn,gn->gt", powers, mode_weight, precision=lax.Precision.HIGHEST)
    toeplitz = toeplitz_from(kernel, block_len)
    decay_into = jnp.exp(-rate[None, :, :] * (lag_float[:, None, None] + 1.0)) * mode_weight[None]
    decay_out = jnp.exp(-rate[None, :, :] * (block_len - 1.0 - lag_float)[:, None, None])
    block_power = jnp.exp(-rate * block_len)
    return (toeplitz, decay_into, decay_out, block_power)


def causal_conv(signal, tables, state_start):
    toeplitz, decay_into, decay_out, block_power = tables
    block_len = toeplitz.shape[1]
    row_count, group_count, group_width = signal.shape
    segments = signal.reshape(row_count // block_len, block_len, group_count, group_width)

    def advance(state_in, segment):
        within = jnp.einsum("gts,sgi->tgi", toeplitz, segment, precision=lax.Precision.HIGHEST)
        carried = jnp.einsum("tgn,gni->tgi", decay_into, state_in, precision=lax.Precision.HIGHEST)
        state_next = block_power[:, :, None] * state_in + jnp.einsum(
            "tgn,tgi->gni", decay_out, segment, precision=lax.Precision.HIGHEST
        )
        return (state_next, within + carried)

    state_end, outputs = lax.scan(advance, state_start, segments)
    return (outputs.reshape(row_count, group_count, group_width), state_end)


def local(projected, short_filter, residue, rate, out_weight):
    row_count = projected.shape[1]
    channels = projected.shape[2]
    group_count = rate.shape[0]
    prior_rows = passed_along(projected[:, -2:, :], "seq", 1)
    extended = jnp.concatenate([prior_rows, projected], axis=1).astype(jnp.float32)
    featured = (
        short_filter[:, 0, None, :] * extended[:, 2:]
        + short_filter[:, 1, None, :] * extended[:, 1 : row_count + 1]
        + short_filter[:, 2, None, :] * extended[:, 0:row_count]
    )
    signal = (featured[1] * featured[2]).reshape(row_count, group_count, GROUP)
    tables = filter_tables(rate, residue, min(256, row_count))
    local_conv, local_end = causal_conv(
        signal, tables, jnp.zeros((group_count, MODES, GROUP), jnp.float32)
    )
    device_power = jnp.exp(-rate * row_count)[:, :, None]

    def relay_state(rounds, received):
        running = device_power * received + local_end
        return passed_along(running, "seq", 1)

    incoming = lax.fori_loop(0, lax.axis_size("seq") - 1, relay_state, jnp.zeros_like(local_end))
    lag_float = lax.iota(jnp.int32, row_count).astype(jnp.float32)
    mode_weight = residue * jnp.sqrt(-jnp.expm1(-2.0 * rate))
    reach = jnp.exp(-rate[None, :, :] * (lag_float[:, None, None] + 1.0)) * mode_weight[None]
    conv = local_conv + jnp.einsum("tgn,gni->tgi", reach, incoming, precision=lax.Precision.HIGHEST)
    mixed = (featured[0] * conv.reshape(row_count, channels)).astype(jnp.bfloat16)
    summed = lax.psum_scatter(
        jnp.dot(mixed, out_weight, preferred_element_type=jnp.float32).astype(jnp.bfloat16),
        "tp",
        scatter_dimension=0,
        tiled=True,
    )
    return summed


def solution(mesh):
    placed = (
        P(None, "seq", "tp"),
        P(None, None, "tp"),
        P("tp", None),
        P("tp", None),
        P("tp", None),
    )
    return jax.shard_map(
        local, mesh=mesh, in_specs=placed, out_specs=P(("seq", "tp"), None), check_vma=False
    )
```

profile of v0, /device:TPU:20, one launch (start us, length us, event | category | flops | bytes accessed | tf_op | source)
XLA Modules:
  0.0 588.9 jit_solution(3185761703311826694)
XLA Ops:
  6.5 0.0 reduce-scatter.2.cloned.1.call-start
  6.5 0.8 slice.37
  7.4 3.4 collective-permute-start.1
  10.8 0.6 convert_add_fusion
  11.4 0.9 fusion.42
  12.3 0.8 copy.25
  13.1 0.8 copy.28
  13.9 0.9 fusion.35
  14.8 0.1 pad.2.clone
  14.9 0.1 maximum_maximum_fusion
  15.0 4.3 tile.4
  19.3 21.5 %copy.44 = f32[8,8,256,512]{3,1,2,0:T(8,128)} copy(f32[8,8,256,512]{3,2,1,0:T(8,128)S(1)} %bitcast.63) | data formatting | bytes 67108864
  40.8 22.5 %slice.54 = f32[64,130816]{1,0:T(8,128)} slice(f32[64,131072]{1,0:T(8,128)} %bitcast.64), slice={[0:64], [0:130816]} | slice | bytes 66977792 | tf_op jit(solution)/shard_map/slice | solution.py:28
  63.4 34.5 %reshape.37 = f32[64,256,511]{2,1,0:T(8,128)} reshape(f32[64,130816]{1,0:T(8,128)} %slice.54) | data formatting | bytes 66977792 | tf_op jit(solution)/shard_map/reshape | solution.py:28
  97.9 14.5 %slice_bitcast_fusion = f32[64,256,256]{1,2,0:T(8,128)} fusion(f32[64,256,511]{2,1,0:T(8,128)} %reshape.37), kind=kLoop, calls=%fused_computation.24 | loop fusion | bytes 33554432 | tf_op jit(solution)/shard_map/transpose | solution.py:30
  112.4 17.4 %copy.30 = f32[64,256,256]{2,1,0:T(8,128)} copy(f32[64,256,256]{1,2,0:T(8,128)} %slice_bitcast_fusion) | data formatting | bytes 33554432
  129.9 0.1 copy.32
  130.0 0.0 collective-permute-done.1
  130.0 4.6 maximum_convert_fusion
  134.6 6.4 %fusion.21 = f32[3,1024,1024]{2,1,0:T(8,128)} fusion(f32[3,1026,1024]{2,1,0:T(8,128)S(1)} %maximum_convert_fusion, f32[3,1024]{1,0:T(4,128)S(1)} %get-tuple-element.236, f32[3,1024]{1,0:T(4,128)S(1)} %get-tuple-element.237, f32[3,1024]{1,0:T(4,128)S(1)} %bitcast.69), kind=kLoop, calls=%fused_computation.27 | loop fusion | flops 15728640 | bytes 50368512 | tf_op jit(solution)/shard_map/add | solution.py:71
  141.0 6.7 %slice_multiply_fusion.3 = f32[1,1024,1024]{2,1,0:T(8,128)} fusion(f32[3,1024,1024]{2,1,0:T(8,128)} %fusion.21), kind=kLoop, calls=%fused_computation.32 | loop fusion | flops 1048576 | bytes 12582912 | tf_op jit(solution)/shard_map/mul | solution.py:75
  147.7 5.4 copy.26
  153.1 5.6 mul.154
  158.8 188.0 %while.26 = (s32[]{:T(128)}, f32[64,16,16]{1,2,0:T(8,128)S(1)}, f32[4,256,64,16]{1,0,3,2:T(4,128)}, f32[64,16]{1,0:T(8,128)S(1)}, f32[4,256,64,16]{1,0,3,2:T(4,1...) while((s32[]{:T(128)}, f32[64,16,16]{1,2,0:T(8,128)S(1)}, ...), condition=%wide.region_1.2_spmd.clone.clone.clone, body=%wide.region_0.1_spmd.clone.clone.clone.sunk | while | flops 907083776 | bytes 28526728 | solution.py:60
  158.8 3.3 constant_dynamic-slice_fusion.2
  162.1 17.2 %fusion.59 = f32[64,16,256]{2,1,0:T(8,128)S(1)} fusion(f32[64,256,256]{2,1,0:T(8,128)} %get-tuple-element.355, f32[1,256,64,16]{1,0,3,2:T(1,128)S(1)} %constant_dynamic-slice_fusion.2), kind=kOutput, calls=%fused_computation.13.clone.1 | convolution fusion | flops 805306368 | bytes 18874368 | tf_op jit(solution)/shard_map/while/body/eval_jaxpr/gts,sgi->tgi/dot_general | solution.py:53
  179.3 1.3 fusion.60
  180.5 1.1 copy.59
  181.6 22.7 %dynamic_update_slice.8 = f32[4,256,64,16]{1,0,3,2:T(4,128)} dynamic-update-slice(f32[4,256,64,16]{1,0,3,2:T(4,128)} %get-tuple-element.340, f32[1,256,64,16]{1,0,3,2:T(1,128)S(1)} %copy.59, s32[]{:T(128)} %get-tuple-element.338, s32[]{:T(128)} %constant.17.clone.1..sunk, s32[]{:T(128)} %constant.17.clone.1..sunk, s32[]{:T(128)} %constant.17.clone.1..sunk) | dynamic-update-slice | bytes 2097156 | tf_op jit(solution)/shard_map/while/body/jit(dynamic_update_index_in_dim)/dynamic_update_slice | solution.py:60
  204.3 1.5 fusion.58
  205.8 3.3 constant_dynamic-slice_fusion.2
  209.1 17.2 %fusion.59 = f32[64,16,256]{2,1,0:T(8,128)S(1)} fusion(f32[64,256,256]{2,1,0:T(8,128)} %get-tuple-element.355, f32[1,256,64,16]{1,0,3,2:T(1,128)S(1)} %constant_dynamic-slice_fusion.2), kind=kOutput, calls=%fused_computation.13.clone.1 | convolution fusion | flops 805306368 | bytes 18874368 | tf_op jit(solution)/shard_map/while/body/eval_jaxpr/gts,sgi->tgi/dot_general | solution.py:53
  226.2 1.3 fusion.60
  227.5 1.1 copy.59
  228.6 22.7 %dynamic_update_slice.8 = f32[4,256,64,16]{1,0,3,2:T(4,128)} dynamic-update-slice(f32[4,256,64,16]{1,0,3,2:T(4,128)} %get-tuple-element.340, f32[1,256,64,16]{1,0,3,2:T(1,128)S(1)} %copy.59, s32[]{:T(128)} %get-tuple-element.338, s32[]{:T(128)} %constant.17.clone.1..sunk, s32[]{:T(128)} %constant.17.clone.1..sunk, s32[]{:T(128)} %constant.17.clone.1..sunk) | dynamic-update-slice | bytes 2097156 | tf_op jit(solution)/shard_map/while/body/jit(dynamic_update_index_in_dim)/dynamic_update_slice | solution.py:60
  251.3 1.5 fusion.58
  252.7 3.3 constant_dynamic-slice_fusion.2
  256.1 17.2 %fusion.59 = f32[64,16,256]{2,1,0:T(8,128)S(1)} fusion(f32[64,256,256]{2,1,0:T(8,128)} %get-tuple-element.355, f32[1,256,64,16]{1,0,3,2:T(1,128)S(1)} %constant_dynamic-slice_fusion.2), kind=kOutput, calls=%fused_computation.13.clone.1 | convolution fusion | flops 805306368 | bytes 18874368 | tf_op jit(solution)/shard_map/while/body/eval_jaxpr/gts,sgi->tgi/dot_general | solution.py:53
  273.2 1.3 fusion.60
  274.5 1.1 copy.59
  275.6 22.7 %dynamic_update_slice.8 = f32[4,256,64,16]{1,0,3,2:T(4,128)} dynamic-update-slice(f32[4,256,64,16]{1,0,3,2:T(4,128)} %get-tuple-element.340, f32[1,256,64,16]{1,0,3,2:T(1,128)S(1)} %copy.59, s32[]{:T(128)} %get-tuple-element.338, s32[]{:T(128)} %constant.17.clone.1..sunk, s32[]{:T(128)} %constant.17.clone.1..sunk, s32[]{:T(128)} %constant.17.clone.1..sunk) | dynamic-update-slice | bytes 2097156 | tf_op jit(solution)/shard_map/while/body/jit(dynamic_update_index_in_dim)/dynamic_update_slice | solution.py:60
  298.2 1.5 fusion.58
  299.7 3.3 constant_dynamic-slice_fusion.2
  303.1 17.2 %fusion.59 = f32[64,16,256]{2,1,0:T(8,128)S(1)} fusion(f32[64,256,256]{2,1,0:T(8,128)} %get-tuple-element.355, f32[1,256,64,16]{1,0,3,2:T(1,128)S(1)} %constant_dynamic-slice_fusion.2), kind=kOutput, calls=%fused_computation.13.clone.1 | convolution fusion | flops 805306368 | bytes 18874368 | tf_op jit(solution)/shard_map/while/body/eval_jaxpr/gts,sgi->tgi/dot_general | solution.py:53
  320.2 1.3 fusion.60
  321.5 1.1 copy.59
  322.6 22.7 %dynamic_update_slice.8 = f32[4,256,64,16]{1,0,3,2:T(4,128)} dynamic-update-slice(f32[4,256,64,16]{1,0,3,2:T(4,128)} %get-tuple-element.340, f32[1,256,64,16]{1,0,3,2:T(1,128)S(1)} %copy.59, s32[]{:T(128)} %get-tuple-element.338, s32[]{:T(128)} %constant.17.clone.1..sunk, s32[]{:T(128)} %constant.17.clone.1..sunk, s32[]{:T(128)} %constant.17.clone.1..sunk) | dynamic-update-slice | bytes 2097156 | tf_op jit(solution)/shard_map/while/body/jit(dynamic_update_index_in_dim)/dynamic_update_slice | solution.py:60
  345.2 1.5 fusion.58
  346.7 0.3 copy.33
  347.0 23.4 %while.25 = (s32[]{:T(128)}, f32[64,16,16]{0,2,1:T(8,128)S(1)}, f32[64,16,1]{0,1,2:T(8,128)S(1)}, f32[64,16,16]{0,2,1:T(8,128)S(1)}, s32[]{:T(128)}) while((s32[]{:T(128)}, f32[64,16,16]{0,2,1:T(8,128)S(1)}, f32[64,16,1]{0,1,2:T(8,128)S(1)}, f32[64,16,16]{0,2,1:T(8,128)S(1)}, s32[]{:T(128)}) %tuple.56), condition=%wide.region_3.4_spmd, body=%wide.region_2.3_spmd.sunk | while | flops 32770 | bytes 462949 | solution.py:86
  347.1 1.9 collective-permute-start
  349.0 5.8 collective-permute-done
  354.8 1.9 collective-permute-start
  356.8 5.8 collective-permute-done
  362.6 1.9 collective-permute-start
  364.6 5.8 collective-permute-done
  370.4 0.3 copy.34
  370.7 6.0 %reshape.38 = f32[1024,64,16]{0,2,1:T(8,128)} reshape(f32[4,256,64,16]{1,0,3,2:T(4,128)} %get-tuple-element.70) | data formatting | bytes 8388608 | tf_op jit(solution)/shard_map/reshape | solution.py:61
  376.7 0.0 copy-done
  376.7 7.0 %bitcast_add_fusion = f32[1024,64,16]{0,2,1:T(8,128)} fusion(f32[1024,64,16]{0,2,1:T(8,128)} %reshape.38, f32[64,16,16]{1,2,0:T(8,128)S(1)} %copy.34, f32[64,16]{1,0:T(8,128)S(1)} %get-tuple-element.383, f32[1024]{0:T(1024)S(1)} %copy-done, f32[64,16]{1,0:T(8,128)S(1)} %get-tuple-element.381), kind=kOutput, calls=%fused_computation.36 | convolution fusion | flops 204472320 | bytes 8466432 | tf_op jit(solution)/shard_map/tgn,gni->tgi/dot_general | solution.py:90
  383.7 5.3 copy.35
  389.1 27.1 %convolution_convert_fusion = bf16[1024,8192]{1,0:T(8,128)(2,1)} fusion(bf16[1024,8192]{1,0:T(8,128)(2,1)} %param.13, f32[1024,1024]{1,0:T(8,128)} %copy.35, f32[3,1024,1024]{2,1,0:T(8,128)} %fusion.21), kind=kOutput, calls=%fused_computation.25 | convolution fusion | flops 17190354944 | bytes 41943040 | tf_op jit(solution)/shard_map/dot_general | solution.py:93
  416.1 0.0 reduce-scatter.2.cloned.1.call-update
  416.2 165.9 %reduce-scatter.2.cloned.1.call-done = bf16[128,8192]{1,0:T(8,128)(2,1)} async-done(((bf16[1024,8192]{1,0:T(8,128)(2,1)}), bf16[128,8192]{1,0:T(8,128)(2,1)}) %reduce-scatter.2.cloned.1.call-update) | async-done | bytes 2097168 | tf_op jit(solution)/shard_map/reduce_scatter | solution.py:92
  (15 shorter events, 0.2 us)
Async XLA Ops:
  6.5 575.5 %reduce-scatter.2.cloned.1.call-start = ((), (), s32[]{:S(2)}) async-start(), calls=%async_computation.1 | async-start | bytes 18874368 | tf_op jit(solution)/shard_map/reduce_scatter | solution.py:92
  7.4 122.6 %collective-permute-start.1 = (bf16[3,2,1024]{2,1,0:T(2,128)(2,1)S(1)}, bf16[3,2,1024]{2,1,0:T(2,128)(2,1)S(1)}, u32[]{:S(2)}, u32[]{:S(2)}) collective-permute-start(bf16[3,2,1024]{2,1,0:T(2,128)(2,1)S(1)} %slice.37), channel_id=1, source_target_pairs={{0,8},{8,16},{16,24},{1,9},{9,17},{17,25},{2,10},{10,18},{18,26},{... | collective-permute-start | bytes 36872 | tf_op jit(solution)/shard_map/ppermute | solution.py:13
  158.8 217.9 %copy-start = (f32[1024]{0:T(1024)S(1)}, f32[1024]{0:T(1024)}, u32[]{:S(2)}) copy-start(f32[1024]{0:T(1024)} %convert_add_fusion) | copy-start | bytes 12292
  347.1 7.8 %collective-permute-start = (f32[64,16,16]{0,2,1:T(8,128)S(1)}, f32[64,16,16]{0,2,1:T(8,128)S(1)}, u32[]{:S(2)}, u32[]{:S(2)}) collective-permute-start(f32[64,16,16]{0,2,1:T(8,128)S(1)} %multiply_add_fusion.2), channel_id=1, source_target_pairs={{0,8},{8,16},{16,24},{1,9},{9,17},{17,25},{2,10},{10,18},{18,26},{... | collective-permute-start | bytes 196616 | tf_op jit(solution)/shard_map/while/body/eval_jaxpr/ppermute | solution.py:13
  354.8 7.8 %collective-permute-start = (f32[64,16,16]{0,2,1:T(8,128)S(1)}, f32[64,16,16]{0,2,1:T(8,128)S(1)}, u32[]{:S(2)}, u32[]{:S(2)}) collective-permute-start(f32[64,16,16]{0,2,1:T(8,128)S(1)} %multiply_add_fusion.2), channel_id=1, source_target_pairs={{0,8},{8,16},{16,24},{1,9},{9,17},{17,25},{2,10},{10,18},{18,26},{... | collective-permute-start | bytes 196616 | tf_op jit(solution)/shard_map/while/body/eval_jaxpr/ppermute | solution.py:13
  362.6 7.8 %collective-permute-start = (f32[64,16,16]{0,2,1:T(8,128)S(1)}, f32[64,16,16]{0,2,1:T(8,128)S(1)}, u32[]{:S(2)}, u32[]{:S(2)}) collective-permute-start(f32[64,16,16]{0,2,1:T(8,128)S(1)} %multiply_add_fusion.2), channel_id=1, source_target_pairs={{0,8},{8,16},{16,24},{1,9},{9,17},{17,25},{2,10},{10,18},{18,26},{... | collective-permute-start | bytes 196616 | tf_op jit(solution)/shard_map/while/body/eval_jaxpr/ppermute | solution.py:13
Sparse Core Ops, SparseCore 0:
  416.3 165.7 reduce-scatter.1
where the time goes:
time: 597 us; the launch traced here: 589 us
  local copies, waits for them, and re-layouts  249 us (42%)
  waiting for transfers between devices  183 us (31%)
  matrix products  115 us (19%)
  other arithmetic  18.6 us (3%)
  between operations  13.5 us (2%)
  starting transfers between devices  9.16 us (2%)
    reduce_scatter x1, waiting for transfers between devices, local(): lax.psum_scatter(jnp.dot(mixed, out_weight, preferred_element_type=jnp.fl...  166 us
    dynamic_update_slice x8, local copies, waits for them, and re-layouts, causal_conv(): state_end, outputs = lax.scan(advance, state_start, segments)  94.9 us
    dot_general x4, matrix products, advance(): jnp.einsum('gts,sgi->tgi', toeplitz, segment, precision=lax.Precision.HIG...  68.6 us
    unnamed x8, local copies, waits for them, and re-layouts  40.5 us
    reshape x1, local copies, waits for them, and re-layouts, toeplitz_from(): tiled[:, :block_len * width].reshape(group_count, block_len, width)  34.5 us
    dot_general x1, matrix products, local(): jnp.dot(mixed, out_weight, preferred_element_type=jnp.float32)  27.1 us
    slice x1, local copies, waits for them, and re-layouts, toeplitz_from(): tiled[:, :block_len * width].reshape(group_count, block_len, width)  22.5 us
    ppermute x4, waiting for transfers between devices, passed_along(): lax.ppermute(value, axis, [(source, source + steps) for source in range(l...  17.5 us
  transfers between devices with their start and end apart: 5, of which 4 were waited for; matrix products, arithmetic and copies ran while one was open for 20% of the time, Pallas kernels for 0%

commit v1 on v0

--- a/solution.py
+++ b/solution.py
@@ -1,10 +1,13 @@
 import jax
 import jax.numpy as jnp
 from jax import lax
+from jax.experimental import pallas as pl
+from jax.experimental.pallas import tpu as pltpu
 from jax.sharding import PartitionSpec as P
 
 GROUP = 16
 MODES = 16
+MESH = pl.DeviceIdType.MESH
 
 
 def passed_along(value, axis, steps):
@@ -61,6 +64,269 @@
     return (outputs.reshape(row_count, group_count, group_width), state_end)
 
 
+def tile_count(chips):
+    return max(1, 32 // chips)
+
+
+def project_and_scatter(mixed, out_weight):
+    tokens, depth = mixed.shape
+    width = out_weight.shape[1]
+    ranks = lax.axis_size("tp")
+    chips = ranks // 2
+    rows = tokens // ranks
+    tiles = tile_count(chips)
+    cols = width // tiles
+    piece = min(256, cols)
+    lag = 2
+    slots = (chips - 1) * tiles
+
+    def kernel(mixed_ref, w_ref, out_ref, w_buf, acc, stage, sib, inc,
+               w_sem, sib_send, sib_recv, fwd_send, in_recv, out_sem):
+        rank = lax.axis_index("tp")
+        z = lax.div(rank, 2)
+        core = lax.rem(rank, 2)
+        partner = z * 2 + (1 - core)
+        above = rank + 2
+        below = rank - 2
+
+        def w_copy(i):
+            return pltpu.make_async_copy(
+                w_ref.at[:, pl.ds(pl.multiple_of(i * cols, cols), cols)], w_buf.at[i], w_sem.at[i]
+            )
+
+        @pl.loop(0, tiles)
+        def _(i):
+            w_copy(i).start()
+
+        barrier = pltpu.get_barrier_semaphore()
+        pl.semaphore_signal(barrier, inc=1, device_id={"tp": partner}, device_id_type=MESH)
+
+        @pl.when(z < chips - 1)
+        def _():
+            pl.semaphore_signal(barrier, inc=1, device_id={"tp": above}, device_id_type=MESH)
+
+        @pl.when(z > 0)
+        def _():
+            pl.semaphore_signal(barrier, inc=1, device_id={"tp": below}, device_id_type=MESH)
+
+        middle = jnp.logical_and(z > 0, z < chips - 1)
+
+        @pl.when(middle)
+        def _():
+            pl.semaphore_wait(barrier, 3)
+
+        @pl.when(jnp.logical_not(middle))
+        def _():
+            pl.semaphore_wait(barrier, 2)
+
+        def sib_copy(dest, i):
+            return pltpu.make_async_remote_copy(
+                src_ref=stage.at[dest, i], dst_ref=sib.at[dest, i],
+                send_sem=sib_send.at[dest, i], recv_sem=sib_recv.at[dest, i],
+                device_id={"tp": partner}, device_id_type=MESH,
+            )
+
+        def fwd_copy(dest, i, landing, target):
+            return pltpu.make_async_remote_copy(
+                src_ref=acc.at[dest, i], dst_ref=inc.at[landing, i],
+                send_sem=fwd_send.at[dest, i], recv_sem=in_recv.at[landing, i],
+                device_id={"tp": target}, device_id_type=MESH,
+            )
+
+        def compute(dest, i):
+            base = dest * (2 * rows)
+            own = mixed_ref[pl.ds(pl.multiple_of(base + core * rows, rows), rows), :]
+            other = mixed_ref[pl.ds(pl.multiple_of(base + (1 - core) * rows, rows), rows), :]
+            left = jnp.concatenate([own, other], axis=0)
+
+            @pl.loop(0, cols // piece)
+            def _(p):
+                at = pl.ds(pl.multiple_of(p * piece, piece), piece)
+                product = jnp.dot(left, w_buf[i, :, at], preferred_element_type=jnp.float32)
+                acc[dest, i, :, at] = product[:rows].astype(jnp.bfloat16)
+                stage[dest, i, :, at] = product[rows:].astype(jnp.bfloat16)
+
+            sib_copy(dest, i).start()
+
+        def add_in(dest, i, landing):
+            @pl.loop(0, cols // piece)
+            def _(p):
+                at = pl.ds(pl.multiple_of(p * piece, piece), piece)
+                total = acc[dest, i, :, at].astype(jnp.float32) + inc[landing, i, :, at].astype(jnp.float32)
+                acc[dest, i, :, at] = (total + sib[dest, i, :, at].astype(jnp.float32)).astype(jnp.bfloat16)
+
+        def add_sib(dest, i):
+            @pl.loop(0, cols // piece)
+            def _(p):
+                at = pl.ds(pl.multiple_of(p * piece, piece), piece)
+                total = acc[dest, i, :, at].astype(jnp.float32) + sib[dest, i, :, at].astype(jnp.float32)
+                acc[dest, i, :, at] = total.astype(jnp.bfloat16)
+
+        def up_place(k):
+            return chips - 1 - lax.div(k, tiles), lax.rem(k, tiles)
+
+        def down_place(k):
+            return lax.div(k, tiles), lax.rem(k, tiles)
+
+        up_count = (chips - 1 - z) * tiles
+        down_count = z * tiles
+        up_shift = z * lag
+        down_shift = (chips - 1 - z) * lag
+        up_first = jnp.where(z < chips - 1, up_shift, slots + lag * chips)
+        down_first = jnp.where(z > 0, down_shift, slots + lag * chips)
+        first = jnp.minimum(up_first, down_first)
+
+        def forward(k, place, fed, landing_of, target):
+            dest, i = place(k)
+
+            @pl.when(k >= 2)
+            def _():
+                before, j = place(k - 2)
+                fwd_copy(before, j, landing_of(before), target).wait_send()
+
+            sib_copy(dest, i).wait_recv()
+
+            @pl.when(fed)
+            def _():
+                fwd_copy(dest, i, dest, target).wait_recv()
+                add_in(dest, i, dest)
+
+            @pl.when(jnp.logical_not(fed))
+            def _():
+                add_sib(dest, i)
+
+            fwd_copy(dest, i, landing_of(dest), target).start()
+
+        def up_landing(dest):
+            return dest
+
+        def down_landing(dest):
+            return jnp.where(dest == z - 1, chips, dest)
+
+        @pl.loop(0, slots + 1)
+        def _(it):
+            w_at = it - first
+
+            @pl.when(jnp.logical_and(w_at >= 0, w_at < tiles))
+            def _():
+                w_copy(w_at).wait()
+
+            ku = it - up_shift
+
+            @pl.when(jnp.logical_and(ku >= 0, ku < up_count))
+            def _():
+                dest, i = up_place(ku)
+                compute(dest, i)
+
+            kd = it - down_shift
+
+            @pl.when(jnp.logical_and(kd >= 0, kd < down_count))
+            def _():
+                dest, i = down_place(kd)
+                compute(dest, i)
+
+            ks = it - first - tiles
+
+            @pl.when(jnp.logical_and(ks >= 0, ks < tiles))
+            def _():
+                compute(z, ks)
+
+            @pl.when(jnp.logical_and(ku >= 1, ku <= up_count))
+            def _():
+                forward(ku - 1, up_place, z > 0, up_landing, above)
+
+            @pl.when(jnp.logical_and(kd >= 1, kd <= down_count))
+            def _():
+                forward(kd - 1, down_place, z < chips - 1, down_landing, below)
+
+        def drain(count, place, landing_of, target):
+            @pl.when(count >= 2)
+            def _():
+                for back in (2, 1):
+                    dest, i = place(count - back)
+                    fwd_copy(dest, i, landing_of(dest), target).wait_send()
+
+            @pl.when(count == 1)
+            def _():
+                dest, i = place(count - 1)
+                fwd_copy(dest, i, landing_of(dest), target).wait_send()
+
+        def out_copy(i):
+            return pltpu.make_async_copy(
+                acc.at[z, i], out_ref.at[:, pl.ds(pl.multiple_of(i * cols, cols), cols)], out_sem.at[i]
+            )
+
+        @pl.loop(0, tiles)
+        def _(i):
+            sib_copy(z, i).wait_recv()
+
+            @pl.when(z < chips - 1)
+            def _():
+                fwd_copy(z, i, chips, above).wait_recv()
+
+            @pl.when(z > 0)
+            def _():
+                fwd_copy(z, i, z, below).wait_recv()
+
+            @pl.when(z == 0)
+            def _():
+                add_in(z, i, chips)
+
+            @pl.when(z == chips - 1)
+            def _():
+                add_in(z, i, z)
+
+            @pl.when(middle)
+            def _():
+                @pl.loop(0, cols // piece)
+                def _(p):
+                    at = pl.ds(pl.multiple_of(p * piece, piece), piece)
+                    total = acc[z, i, :, at].astype(jnp.float32) + sib[z, i, :, at].astype(jnp.float32)
+                    total = total + inc[z, i, :, at].astype(jnp.float32)
+                    total = total + inc[chips, i, :, at].astype(jnp.float32)
+                    acc[z, i, :, at] = total.astype(jnp.bfloat16)
+
+            out_copy(i).start()
+
+        drain(up_count, up_place, up_landing, above)
+        drain(down_count, down_place, down_landing, below)
+
+        @pl.loop(0, tiles)
+        def _(i):
+            out_copy(i).wait()
+
+            @pl.loop(0, chips)
+            def _(dest):
+                sib_copy(dest, i).wait_send()
+
+    block = (chips, tiles, rows, cols)
+    return pl.pallas_call(
+        kernel,
+        out_shape=jax.ShapeDtypeStruct((rows, width), jnp.bfloat16),
+        in_specs=[pl.BlockSpec(memory_space=pltpu.VMEM), pl.BlockSpec(memory_space=pl.ANY)],
+        out_specs=pl.BlockSpec(memory_space=pl.ANY),
+        scratch_shapes=[
+            pltpu.VMEM((tiles, depth, cols), jnp.bfloat16),
+            pltpu.VMEM(block, jnp.bfloat16),
+            pltpu.VMEM(block, jnp.bfloat16),
+            pltpu.VMEM(block, jnp.bfloat16),
+            pltpu.VMEM((chips + 1, tiles, rows, cols), jnp.bfloat16),
+            pltpu.SemaphoreType.DMA((tiles,)),
+            pltpu.SemaphoreType.DMA((chips, tiles)),
+            pltpu.SemaphoreType.DMA((chips, tiles)),
+            pltpu.SemaphoreType.DMA((chips, tiles)),
+            pltpu.SemaphoreType.DMA((chips + 1, tiles)),
+            pltpu.SemaphoreType.DMA((tiles,)),
+        ],
+        compiler_params=pltpu.CompilerParams(
+            collective_id=0, has_side_effects=True, vmem_limit_bytes=60 * 1024 * 1024
+        ),
+        cost_estimate=pl.CostEstimate(
+            flops=2 * tokens * depth * width, bytes_accessed=2 * depth * width, transcendentals=0
+        ),
+    )(mixed, out_weight)
+
+
 def local(projected, short_filter, residue, rate, out_weight):
     row_count = projected.shape[1]
     channels = projected.shape[2]
@@ -89,13 +355,7 @@
     reach = jnp.exp(-rate[None, :, :] * (lag_float[:, None, None] + 1.0)) * mode_weight[None]
     conv = local_conv + jnp.einsum("tgn,gni->tgi", reach, incoming, precision=lax.Precision.HIGHEST)
     mixed = (featured[0] * conv.reshape(row_count, channels)).astype(jnp.bfloat16)
-    summed = lax.psum_scatter(
-        jnp.dot(mixed, out_weight, preferred_element_type=jnp.float32).astype(jnp.bfloat16),
-        "tp",
-        scatter_dimension=0,
-        tiled=True,
-    )
-    return summed
+    return project_and_scatter(mixed, out_weight)
 
 
 def solution(mesh):

time: 597 us -> 540 us (0.905)
  waiting for transfers between devices: 183 us -> 17.5 us
  Pallas kernels: 0 us -> 146 us
  matrix products: 115 us -> 87.5 us
  between operations: 13.5 us -> 0.17 us
    reduce_scatter x1 -> x0, waiting for transfers between devices: 166 us -> none  [local(): lax.psum_scatter(jnp.dot(mixed, out_weight, preferred_element_type=jnp.fl...]
    pallas_call x0 -> x1, Pallas kernels: none -> 146 us  [project_and_scatter(): pl.pallas_call(kernel, out_shape=jax.ShapeDtypeStruct((rows, width), jnp....]
    dot_general x1 -> x0, matrix products: 27.1 us -> none  [local(): jnp.dot(mixed, out_weight, preferred_element_type=jnp.float32)]
    unnamed x8 -> x9, local copies, waits for them, and re-layouts: 40.5 us -> 43.6 us
  transfers between devices with their start and end apart: 5 -> 4, of which waited for: 4 -> 3; matrix products, arithmetic and copies ran while one was open for 20% -> 22% of each run, Pallas kernels for 0% -> 0%
where the time goes in v1:
time: 540 us; the launch traced here: 537 us
  local copies, waits for them, and re-layouts  253 us (47%)
  Pallas kernels  146 us (27%)
  matrix products  87.5 us (16%)
  other arithmetic  24.1 us (4%)
  waiting for transfers between devices  17.5 us (3%)
  starting transfers between devices  9.16 us (2%)
    pallas_call x1, Pallas kernels, project_and_scatter(): pl.pallas_call(kernel, out_shape=jax.ShapeDtypeStruct((rows, width), jnp....  146 us
    dynamic_update_slice x8, local copies, waits for them, and re-layouts, causal_conv(): state_end, outputs = lax.scan(advance, state_start, segments)  95 us
    dot_general x4, matrix products, advance(): jnp.einsum('gts,sgi->tgi', toeplitz, segment, precision=lax.Precision.HIG...  68.6 us
    unnamed x9, local copies, waits for them, and re-layouts  43.6 us
    reshape x1, local copies, waits for them, and re-layouts, toeplitz_from(): tiled[:, :block_len * width].reshape(group_count, block_len, width)  34.5 us
    slice x1, local copies, waits for them, and re-layouts, toeplitz_from(): tiled[:, :block_len * width].reshape(group_count, block_len, width)  22.5 us
    ppermute x4, waiting for transfers between devices, passed_along(): lax.ppermute(value, axis, [(source, source + steps) for source in range(l...  17.5 us
    transpose x1, local copies, waits for them, and re-layouts, toeplitz_from(): return jnp.swapaxes(hankel, 1, 2)  14.5 us
  transfers between devices with their start and end apart: 4, of which 3 were waited for; matrix products, arithmetic and copies ran while one was open for 22% of the time, Pallas kernels for 0%

profile of v1, /device:TPU:20, one launch (start us, length us, event | category | flops | bytes accessed | tf_op | source)
XLA Modules:
  0.0 536.9 jit_solution(12378654602157273311)
XLA Ops:
  0.0 0.8 slice.37
  0.8 3.4 collective-permute-start.1
  4.2 0.6 convert_add_fusion
  4.8 0.9 fusion.41
  5.8 0.8 copy.26
  6.6 0.8 copy.29
  7.4 0.9 fusion.34
  8.3 0.1 pad.2.clone
  8.4 0.1 maximum_maximum_fusion
  8.5 4.3 tile.4
  12.8 21.5 %copy.45 = f32[8,8,256,512]{3,1,2,0:T(8,128)} copy(f32[8,8,256,512]{3,2,1,0:T(8,128)S(1)} %bitcast.61) | data formatting | bytes 67108864
  34.3 22.5 %slice.54 = f32[64,130816]{1,0:T(8,128)} slice(f32[64,131072]{1,0:T(8,128)} %bitcast.62), slice={[0:64], [0:130816]} | slice | bytes 66977792 | tf_op jit(solution)/shard_map/slice | solution.py:31
  56.8 34.5 %reshape.37 = f32[64,256,511]{2,1,0:T(8,128)} reshape(f32[64,130816]{1,0:T(8,128)} %slice.54) | data formatting | bytes 66977792 | tf_op jit(solution)/shard_map/reshape | solution.py:31
  91.4 14.5 %slice_bitcast_fusion = f32[64,256,256]{1,2,0:T(8,128)} fusion(f32[64,256,511]{2,1,0:T(8,128)} %reshape.37), kind=kLoop, calls=%fused_computation.24 | loop fusion | bytes 33554432 | tf_op jit(solution)/shard_map/transpose | solution.py:33
  105.9 17.4 %copy.31 = f32[64,256,256]{2,1,0:T(8,128)} copy(f32[64,256,256]{1,2,0:T(8,128)} %slice_bitcast_fusion) | data formatting | bytes 33554432
  123.4 0.1 copy.33
  123.4 0.0 collective-permute-done.1
  123.4 4.6 maximum_convert_fusion
  128.1 6.4 %fusion.21 = f32[3,1024,1024]{2,1,0:T(8,128)} fusion(f32[3,1026,1024]{2,1,0:T(8,128)S(1)} %maximum_convert_fusion, f32[3,1024]{1,0:T(4,128)S(1)} %get-tuple-element.246, f32[3,1024]{1,0:T(4,128)S(1)} %get-tuple-element.247, f32[3,1024]{1,0:T(4,128)S(1)} %bitcast.67), kind=kLoop, calls=%fused_computation.26 | loop fusion | flops 15728640 | bytes 50368512 | tf_op jit(solution)/shard_map/add | solution.py:337
  134.4 6.8 %slice_multiply_fusion.3 = f32[1,1024,1024]{2,1,0:T(8,128)} fusion(f32[3,1024,1024]{2,1,0:T(8,128)} %fusion.21), kind=kLoop, calls=%fused_computation.31 | loop fusion | flops 1048576 | bytes 12582912 | tf_op jit(solution)/shard_map/mul | solution.py:341
  141.2 5.4 %copy.27 = f32[1,1024,1024]{1,2,0:T(8,128)} copy(f32[1,1024,1024]{2,1,0:T(8,128)} %slice_multiply_fusion.3) | data formatting | bytes 8388608 | tf_op jit(solution)/shard_map/mul | solution.py:341
  146.6 5.6 %mul.154 = f32[4,256,64,16]{1,0,3,2:T(4,128)} reshape(f32[1,1024,1024]{1,2,0:T(8,128)} %copy.27) | data formatting | bytes 8388608 | tf_op jit(solution)/shard_map/mul | solution.py:341
  152.2 188.0 %while.26 = (s32[]{:T(128)}, f32[64,16,16]{1,2,0:T(8,128)S(1)}, f32[4,256,64,16]{1,0,3,2:T(4,128)}, f32[64,16]{1,0:T(8,128)S(1)}, f32[4,256,64,16]{1,0,3,2:T(4,1...) while((s32[]{:T(128)}, f32[64,16,16]{1,2,0:T(8,128)S(1)}, ...), condition=%wide.region_1.2_spmd.clone.clone.clone, body=%wide.region_0.1_spmd.clone.clone.clone.sunk | while | flops 907083776 | bytes 28526728 | solution.py:63
  152.2 3.3 constant_dynamic-slice_fusion.2
  155.6 17.2 %fusion.57 = f32[64,16,256]{2,1,0:T(8,128)S(1)} fusion(f32[64,256,256]{2,1,0:T(8,128)} %get-tuple-element.365, f32[1,256,64,16]{1,0,3,2:T(1,128)S(1)} %constant_dynamic-slice_fusion.2), kind=kOutput, calls=%fused_computation.13.clone.1 | convolution fusion | flops 805306368 | bytes 18874368 | tf_op jit(solution)/shard_map/while/body/eval_jaxpr/gts,sgi->tgi/dot_general | solution.py:56
  172.7 1.3 fusion.58
  174.0 1.1 copy.60
  175.1 22.7 %dynamic_update_slice.8 = f32[4,256,64,16]{1,0,3,2:T(4,128)} dynamic-update-slice(f32[4,256,64,16]{1,0,3,2:T(4,128)} %get-tuple-element.350, f32[1,256,64,16]{1,0,3,2:T(1,128)S(1)} %copy.60, s32[]{:T(128)} %get-tuple-element.348, s32[]{:T(128)} %constant.17.clone.1..sunk, s32[]{:T(128)} %constant.17.clone.1..sunk, s32[]{:T(128)} %constant.17.clone.1..sunk) | dynamic-update-slice | bytes 2097156 | tf_op jit(solution)/shard_map/while/body/jit(dynamic_update_index_in_dim)/dynamic_update_slice | solution.py:63
  197.7 1.5 fusion.56
  199.2 3.3 constant_dynamic-slice_fusion.2
  202.6 17.2 %fusion.57 = f32[64,16,256]{2,1,0:T(8,128)S(1)} fusion(f32[64,256,256]{2,1,0:T(8,128)} %get-tuple-element.365, f32[1,256,64,16]{1,0,3,2:T(1,128)S(1)} %constant_dynamic-slice_fusion.2), kind=kOutput, calls=%fused_computation.13.clone.1 | convolution fusion | flops 805306368 | bytes 18874368 | tf_op jit(solution)/shard_map/while/body/eval_jaxpr/gts,sgi->tgi/dot_general | solution.py:56
  219.7 1.3 fusion.58
  221.0 1.1 copy.60
  222.1 22.7 %dynamic_update_slice.8 = f32[4,256,64,16]{1,0,3,2:T(4,128)} dynamic-update-slice(f32[4,256,64,16]{1,0,3,2:T(4,128)} %get-tuple-element.350, f32[1,256,64,16]{1,0,3,2:T(1,128)S(1)} %copy.60, s32[]{:T(128)} %get-tuple-element.348, s32[]{:T(128)} %constant.17.clone.1..sunk, s32[]{:T(128)} %constant.17.clone.1..sunk, s32[]{:T(128)} %constant.17.clone.1..sunk) | dynamic-update-slice | bytes 2097156 | tf_op jit(solution)/shard_map/while/body/jit(dynamic_update_index_in_dim)/dynamic_update_slice | solution.py:63
  244.8 1.5 fusion.56
  246.2 3.3 constant_dynamic-slice_fusion.2
  249.6 17.2 %fusion.57 = f32[64,16,256]{2,1,0:T(8,128)S(1)} fusion(f32[64,256,256]{2,1,0:T(8,128)} %get-tuple-element.365, f32[1,256,64,16]{1,0,3,2:T(1,128)S(1)} %constant_dynamic-slice_fusion.2), kind=kOutput, calls=%fused_computation.13.clone.1 | convolution fusion | flops 805306368 | bytes 18874368 | tf_op jit(solution)/shard_map/while/body/eval_jaxpr/gts,sgi->tgi/dot_general | solution.py:56
  266.7 1.3 fusion.58
  268.0 1.1 copy.60
  269.1 22.7 %dynamic_update_slice.8 = f32[4,256,64,16]{1,0,3,2:T(4,128)} dynamic-update-slice(f32[4,256,64,16]{1,0,3,2:T(4,128)} %get-tuple-element.350, f32[1,256,64,16]{1,0,3,2:T(1,128)S(1)} %copy.60, s32[]{:T(128)} %get-tuple-element.348, s32[]{:T(128)} %constant.17.clone.1..sunk, s32[]{:T(128)} %constant.17.clone.1..sunk, s32[]{:T(128)} %constant.17.clone.1..sunk) | dynamic-update-slice | bytes 2097156 | tf_op jit(solution)/shard_map/while/body/jit(dynamic_update_index_in_dim)/dynamic_update_slice | solution.py:63
  291.8 1.5 fusion.56
  293.3 3.3 constant_dynamic-slice_fusion.2
  296.6 17.2 %fusion.57 = f32[64,16,256]{2,1,0:T(8,128)S(1)} fusion(f32[64,256,256]{2,1,0:T(8,128)} %get-tuple-element.365, f32[1,256,64,16]{1,0,3,2:T(1,128)S(1)} %constant_dynamic-slice_fusion.2), kind=kOutput, calls=%fused_computation.13.clone.1 | convolution fusion | flops 805306368 | bytes 18874368 | tf_op jit(solution)/shard_map/while/body/eval_jaxpr/gts,sgi->tgi/dot_general | solution.py:56
  313.7 1.3 fusion.58
  315.0 1.1 copy.60
  316.1 22.7 %dynamic_update_slice.8 = f32[4,256,64,16]{1,0,3,2:T(4,128)} dynamic-update-slice(f32[4,256,64,16]{1,0,3,2:T(4,128)} %get-tuple-element.350, f32[1,256,64,16]{1,0,3,2:T(1,128)S(1)} %copy.60, s32[]{:T(128)} %get-tuple-element.348, s32[]{:T(128)} %constant.17.clone.1..sunk, s32[]{:T(128)} %constant.17.clone.1..sunk, s32[]{:T(128)} %constant.17.clone.1..sunk) | dynamic-update-slice | bytes 2097156 | tf_op jit(solution)/shard_map/while/body/jit(dynamic_update_index_in_dim)/dynamic_update_slice | solution.py:63
  338.8 1.5 fusion.56
  340.3 0.0 copy-start
  340.3 0.3 copy.34
  340.6 23.4 %while.25 = (s32[]{:T(128)}, f32[64,16,16]{0,2,1:T(8,128)S(1)}, f32[64,16,1]{0,1,2:T(8,128)S(1)}, f32[64,16,16]{0,2,1:T(8,128)S(1)}, s32[]{:T(128)}) while((s32[]{:T(128)}, f32[64,16,16]{0,2,1:T(8,128)S(1)}, f32[64,16,1]{0,1,2:T(8,128)S(1)}, f32[64,16,16]{0,2,1:T(8,128)S(1)}, s32[]{:T(128)}) %tuple.57), condition=%wide.region_3.4_spmd, body=%wide.region_2.3_spmd.sunk | while | flops 32770 | bytes 462949 | solution.py:352
  340.6 1.9 collective-permute-start
  342.5 5.8 %collective-permute-done = f32[64,16,16]{0,2,1:T(8,128)S(1)} collective-permute-done((f32[64,16,16]{0,2,1:T(8,128)S(1)}, f32[64,16,16]{0,2,1:T(8,128)S(1)}, u32[]{:S(2)}, u32[]{:S(2)}) %collective-permute-start) | collective-permute-done | bytes 65568 | tf_op jit(solution)/shard_map/while/body/eval_jaxpr/ppermute | solution.py:16
  348.4 1.9 collective-permute-start
  350.3 5.8 %collective-permute-done = f32[64,16,16]{0,2,1:T(8,128)S(1)} collective-permute-done((f32[64,16,16]{0,2,1:T(8,128)S(1)}, f32[64,16,16]{0,2,1:T(8,128)S(1)}, u32[]{:S(2)}, u32[]{:S(2)}) %collective-permute-start) | collective-permute-done | bytes 65568 | tf_op jit(solution)/shard_map/while/body/eval_jaxpr/ppermute | solution.py:16
  356.2 1.9 collective-permute-start
  358.1 5.8 %collective-permute-done = f32[64,16,16]{0,2,1:T(8,128)S(1)} collective-permute-done((f32[64,16,16]{0,2,1:T(8,128)S(1)}, f32[64,16,16]{0,2,1:T(8,128)S(1)}, u32[]{:S(2)}, u32[]{:S(2)}) %collective-permute-start) | collective-permute-done | bytes 65568 | tf_op jit(solution)/shard_map/while/body/eval_jaxpr/ppermute | solution.py:16
  363.9 0.3 copy.35
  364.2 6.0 %reshape.38 = f32[1024,64,16]{0,2,1:T(8,128)} reshape(f32[4,256,64,16]{1,0,3,2:T(4,128)} %get-tuple-element.70) | data formatting | bytes 8388608 | tf_op jit(solution)/shard_map/reshape | solution.py:64
  370.3 0.0 copy-done
  370.3 7.1 %bitcast_add_fusion = f32[1024,64,16]{0,2,1:T(8,128)} fusion(f32[1024,64,16]{0,2,1:T(8,128)} %reshape.38, f32[64,16,16]{1,2,0:T(8,128)S(1)} %copy.35, f32[64,16]{1,0:T(8,128)S(1)} %get-tuple-element.390, f32[1024]{0:T(1024)S(1)} %copy-done, f32[64,16]{1,0:T(8,128)S(1)} %get-tuple-element.388), kind=kOutput, calls=%fused_computation.35 | convolution fusion | flops 204472320 | bytes 8466432 | tf_op jit(solution)/shard_map/tgn,gni->tgi/dot_general | solution.py:356
  377.3 5.3 copy.36
  382.7 5.5 %fusion.24.mixed_ref = bf16[1024,1024]{1,0:T(8,128)(2,1)} fusion(f32[1024,1024]{1,0:T(8,128)} %copy.36, f32[3,1024,1024]{2,1,0:T(8,128)} %fusion.21), kind=kLoop, calls=%fused_computation.34 | loop fusion | flops 2097152 | bytes 10485760 | tf_op jit(solution)/shard_map/convert_element_type | solution.py:357
  388.2 145.6 %shard_map.55 = bf16[128,8192]{1,0:T(8,128)(2,1)} custom-call(bf16[1024,1024]{1,0:T(8,128)(2,1)} %fusion.24.mixed_ref, bf16[1024,8192]{1,0:T(8,128)(2,1)} %w_ref.1), custom_call_target="tpu_custom_call" | custom-call | flops 17179869184 | bytes 16777216 | tf_op jit(solution)/shard_map/pallas_call | solution.py:303
  533.8 3.1 copy.80
  (14 shorter events, 0.1 us)
Async XLA Ops:
  0.8 122.6 %collective-permute-start.1 = (bf16[3,2,1024]{2,1,0:T(2,128)(2,1)S(1)}, bf16[3,2,1024]{2,1,0:T(2,128)(2,1)S(1)}, u32[]{:S(2)}, u32[]{:S(2)}) collective-permute-start(bf16[3,2,1024]{2,1,0:T(2,128)(2,1)S(1)} %slice.37), channel_id=1, source_target_pairs={{0,8},{8,16},{16,24},{1,9},{9,17},{17,25},{2,10},{10,18},{18,26},{... | collective-permute-start | bytes 36872 | tf_op jit(solution)/shard_map/ppermute | solution.py:16
  340.3 30.0 %copy-start = (f32[1024]{0:T(1024)S(1)}, f32[1024]{0:T(1024)}, u32[]{:S(2)}) copy-start(f32[1024]{0:T(1024)} %convert_add_fusion) | copy-start | bytes 12292
  340.6 7.8 %collective-permute-start = (f32[64,16,16]{0,2,1:T(8,128)S(1)}, f32[64,16,16]{0,2,1:T(8,128)S(1)}, u32[]{:S(2)}, u32[]{:S(2)}) collective-permute-start(f32[64,16,16]{0,2,1:T(8,128)S(1)} %multiply_add_fusion.2), channel_id=1, source_target_pairs={{0,8},{8,16},{16,24},{1,9},{9,17},{17,25},{2,10},{10,18},{18,26},{... | collective-permute-start | bytes 196616 | tf_op jit(solution)/shard_map/while/body/eval_jaxpr/ppermute | solution.py:16
  348.4 7.8 %collective-permute-start = (f32[64,16,16]{0,2,1:T(8,128)S(1)}, f32[64,16,16]{0,2,1:T(8,128)S(1)}, u32[]{:S(2)}, u32[]{:S(2)}) collective-permute-start(f32[64,16,16]{0,2,1:T(8,128)S(1)} %multiply_add_fusion.2), channel_id=1, source_target_pairs={{0,8},{8,16},{16,24},{1,9},{9,17},{17,25},{2,10},{10,18},{18,26},{... | collective-permute-start | bytes 196616 | tf_op jit(solution)/shard_map/while/body/eval_jaxpr/ppermute | solution.py:16
  356.2 7.8 %collective-permute-start = (f32[64,16,16]{0,2,1:T(8,128)S(1)}, f32[64,16,16]{0,2,1:T(8,128)S(1)}, u32[]{:S(2)}, u32[]{:S(2)}) collective-permute-start(f32[64,16,16]{0,2,1:T(8,128)S(1)} %multiply_add_fusion.2), channel_id=1, source_target_pairs={{0,8},{8,16},{16,24},{1,9},{9,17},{17,25},{2,10},{10,18},{18,26},{... | collective-permute-start | bytes 196616 | tf_op jit(solution)/shard_map/while/body/eval_jaxpr/ppermute | solution.py:16

commit v2 on v1

--- a/solution.py
+++ b/solution.py
@@ -8,60 +8,219 @@
 GROUP = 16
 MODES = 16
 MESH = pl.DeviceIdType.MESH
-
-
-def passed_along(value, axis, steps):
-    count = lax.axis_size(axis)
-    leading, last = (max(0, -steps), min(count, count - steps))
-    return lax.ppermute(value, axis, [(source, source + steps) for source in range(leading, last)])
-
-
-def toeplitz_from(kernel, block_len):
-    group_count = kernel.shape[0]
-    padded = jnp.concatenate(
-        [
-            jnp.zeros((group_count, block_len - 1), jnp.float32),
-            kernel,
-            jnp.zeros((group_count, 1), jnp.float32),
+WINDOW = 32
+LANES = 128
+
+
+def split(value):
+    high = value.astype(jnp.bfloat16)
+    return high, (value - high.astype(jnp.float32)).astype(jnp.bfloat16)
+
+
+def iota(shape, dim):
+    return lax.broadcasted_iota(jnp.int32, shape, dim)
+
+
+def mix(projected, short_filter, residue, rate):
+    tokens, channels = projected.shape[1:]
+    blocks = channels // LANES
+    count = lax.axis_size("seq")
+    chunk = min(256, tokens)
+    chunks = tokens // chunk
+    wide = chunks * LANES
+    held = LANES // GROUP
+    mode_weight = residue * jnp.sqrt(-jnp.expm1(-2.0 * rate))
+    rows = jnp.stack([rate.reshape(blocks, LANES), mode_weight.reshape(blocks, LANES)], axis=1)
+    down = jnp.broadcast_to(rate.reshape(channels, 1), (channels, LANES))
+
+    def kernel(proj, taps, row_ref, down_ref, out, halo, ext, table, q_buf, x_buf, s_buf, y_buf,
+               end, landed, state, halo_send, halo_recv, end_send, end_recv):
+        me = lax.axis_index("seq")
+
+        barrier = pltpu.get_barrier_semaphore()
+
+        @pl.loop(1, count)
+        def _(k):
+            pl.semaphore_signal(
+                barrier, inc=1, device_id={"seq": lax.rem(me + k, count)}, device_id_type=MESH
+            )
+
+        pl.semaphore_wait(barrier, count - 1)
+
+        def halo_copy(target):
+            return pltpu.make_async_remote_copy(
+                src_ref=proj.at[:, pl.ds(tokens - 16, 16), :], dst_ref=halo,
+                send_sem=halo_send, recv_sem=halo_recv,
+                device_id={"seq": target}, device_id_type=MESH,
+            )
+
+        def end_copy(slot, k, target):
+            return pltpu.make_async_remote_copy(
+                src_ref=end, dst_ref=landed.at[slot],
+                send_sem=end_send.at[k], recv_sem=end_recv.at[slot],
+                device_id={"seq": target}, device_id_type=MESH,
+            )
+
+        @pl.when(me < count - 1)
+        def _():
+            halo_copy(me + 1).start()
+
+        @pl.loop(0, blocks)
+        def _(b):
+            rate_row = row_ref[b, 0:1, :]
+            weight_row = row_ref[b, 1:2, :]
+            lag = iota((chunk, LANES), 0).astype(jnp.float32) - (WINDOW - 1.0)
+            p_high, p_low = split(jnp.exp(-rate_row * lag) * weight_row)
+            rate_down = down_ref[pl.ds(pl.multiple_of(b * LANES, LANES), LANES), :]
+            rate_down = jnp.concatenate([rate_down] * (held * WINDOW // LANES), axis=1)
+            shape = (LANES, held * WINDOW)
+            place = lax.rem(iota(shape, 1), WINDOW).astype(jnp.float32) - (WINDOW - 1.0)
+            same = lax.div(iota(shape, 0), MODES) == lax.div(iota(shape, 1), WINDOW)
+            g_high, g_low = split(jnp.where(same, jnp.exp(rate_down * place), 0.0))
+            filled = jnp.dot(
+                jnp.concatenate([p_high, p_high, p_low], axis=1),
+                jnp.concatenate([g_high, g_low, g_high], axis=0),
+                preferred_element_type=jnp.float32,
+            )
+            shape = (chunk, held * WINDOW)
+            causal = iota(shape, 0) >= lax.rem(iota(shape, 1), WINDOW)
+            table[b] = jnp.where(causal, filled, 0.0).astype(jnp.bfloat16)
+
+        @pl.when(me > 0)
+        def _():
+            halo_copy(me).wait_recv()
+
+        @pl.when(me == 0)
+        def _():
+            halo[...] = jnp.zeros_like(halo)
+
+        @pl.loop(0, blocks)
+        def _(b):
+            at = pl.ds(pl.multiple_of(b * LANES, LANES), LANES)
+            for p in range(3):
+                ext[p, 0:16, :] = halo[p, :, at].astype(jnp.float32)
+                ext[p, 16 : 16 + tokens, :] = proj[p, :, at].astype(jnp.float32)
+            for c in range(chunks):
+                features = []
+                for p in range(3):
+                    total = None
+                    for j in range(3):
+                        term = taps[p, j : j + 1, at] * ext[p, pl.ds(16 - j + c * chunk, chunk), :]
+                        total = term if total is None else total + term
+                    features.append(total)
+                lanes = slice(c * LANES, (c + 1) * LANES)
+                q_buf[b, :, lanes] = features[0]
+                x_buf[b, :, lanes] = (features[1] * features[2]).astype(jnp.bfloat16)
+            rate_down = down_ref[at, :]
+            rate_wide = jnp.concatenate([rate_down] * (chunk // LANES), axis=1)
+            left = (chunk - 1.0) - iota((LANES, chunk), 1).astype(jnp.float32)
+            e_high, e_low = split(jnp.exp(-rate_wide * left))
+            both = jnp.dot(
+                jnp.concatenate([e_high, e_low], axis=0), x_buf[b], preferred_element_type=jnp.float32
+            )
+            shape = (LANES, wide)
+            same = lax.div(iota(shape, 0), MODES) == lax.div(lax.rem(iota(shape, 1), LANES), GROUP)
+            gained = jnp.where(same, both[:LANES] + both[LANES:], 0.0)
+            s_buf[b] = gained
+            power = jnp.exp(-rate_down * float(chunk))
+            running = gained[:, 0:LANES]
+            for c in range(1, chunks):
+                running = power * running + gained[:, c * LANES : (c + 1) * LANES]
+            packed = running[0:MODES]
+            for g in range(1, held):
+                packed = packed + running[g * MODES : (g + 1) * MODES]
+            end[b] = packed
+
+        @pl.loop(1, count)
+        def _(k):
+            @pl.when(me + k < count)
+            def _():
+                end_copy(me, k, me + k).start()
+
+        @pl.loop(0, blocks)
+        def _(b):
+            y_buf[b] = jnp.zeros((chunk, wide), jnp.float32)
+            lane = lax.div(lax.rem(iota((WINDOW, wide), 1), LANES), GROUP)
+            for w in range(chunk // WINDOW):
+                begin = w * WINDOW
+                piece = x_buf[b, begin : begin + WINDOW, :].astype(jnp.float32)
+                spread = jnp.concatenate(
+                    [jnp.where(lane == g, piece, 0.0).astype(jnp.bfloat16) for g in range(held)], axis=0
+                )
+                y_buf[b, begin:chunk, :] += jnp.dot(
+                    table[b, 0 : chunk - begin, :], spread, preferred_element_type=jnp.float32
+                )
+
+        state[...] = jnp.zeros_like(state)
+
+        @pl.loop(0, count - 1)
+        def _(source):
+            @pl.when(source < me)
+            def _():
+                end_copy(source, 1, me).wait_recv()
+
+                @pl.loop(0, blocks)
+                def _(b):
+                    rate_down = down_ref[pl.ds(pl.multiple_of(b * LANES, LANES), LANES), :]
+                    shape = (LANES, LANES)
+                    same = lax.div(iota(shape, 0), MODES) == lax.div(iota(shape, 1), GROUP)
+                    arrived = jnp.where(same, jnp.concatenate([landed[source, b]] * held, axis=0), 0.0)
+                    state[b] = jnp.exp(-rate_down * float(tokens)) * state[b] + arrived
+
+        @pl.loop(0, blocks)
+        def _(b):
+            at = pl.ds(pl.multiple_of(b * LANES, LANES), LANES)
+            power = jnp.exp(-down_ref[at, :] * float(chunk))
+            states = [state[b]]
+            for c in range(chunks - 1):
+                states.append(power * states[-1] + s_buf[b, :, c * LANES : (c + 1) * LANES])
+            s_high, s_low = split(jnp.concatenate(states, axis=1))
+            lag = iota((chunk, LANES), 0).astype(jnp.float32) + 1.0
+            d_high, d_low = split(jnp.exp(-row_ref[b, 0:1, :] * lag) * row_ref[b, 1:2, :])
+            carried = jnp.dot(
+                jnp.concatenate([d_high, d_high, d_low], axis=1),
+                jnp.concatenate([s_high, s_low, s_high], axis=0),
+                preferred_element_type=jnp.float32,
+            )
+            mixed = (q_buf[b] * (y_buf[b] + carried)).astype(jnp.bfloat16)
+            for c in range(chunks):
+                out[c * chunk : (c + 1) * chunk, at] = mixed[:, c * LANES : (c + 1) * LANES]
+
+        @pl.when(me < count - 1)
+        def _():
+            halo_copy(me + 1).wait_send()
+
+        @pl.loop(1, count)
+        def _(k):
+            @pl.when(me + k < count)
+            def _():
+                end_copy(me, k, me + k).wait_send()
+
+    return pl.pallas_call(
+        kernel,
+        out_shape=jax.ShapeDtypeStruct((tokens, channels), jnp.bfloat16),
+        in_specs=[pl.BlockSpec(memory_space=pltpu.VMEM)] * 4,
+        out_specs=pl.BlockSpec(memory_space=pltpu.VMEM),
+        scratch_shapes=[
+            pltpu.VMEM((3, 16, channels), jnp.bfloat16),
+            pltpu.VMEM((3, 16 + tokens, LANES), jnp.float32),
+            pltpu.VMEM((blocks, chunk, held * WINDOW), jnp.bfloat16),
+            pltpu.VMEM((blocks, chunk, wide), jnp.float32),
+            pltpu.VMEM((blocks, chunk, wide), jnp.bfloat16),
+            pltpu.VMEM((blocks, LANES, wide), jnp.float32),
+            pltpu.VMEM((blocks, chunk, wide), jnp.float32),
+            pltpu.VMEM((blocks, MODES, LANES), jnp.float32),
+            pltpu.VMEM((count, blocks, MODES, LANES), jnp.float32),
+            pltpu.VMEM((blocks, LANES, LANES), jnp.float32),
+            pltpu.SemaphoreType.DMA,
+            pltpu.SemaphoreType.DMA,
+            pltpu.SemaphoreType.DMA((count,)),
+            pltpu.SemaphoreType.DMA((count,)),
         ],
-        axis=1,
-    )
-    tiled = jnp.tile(padded, (1, block_len))
-    width = 2 * block_len - 1
-    trimmed = tiled[:, : block_len * width].reshape(group_count, block_len, width)
-    hankel = trimmed[:, :, block_len - 1 : width]
-    return jnp.swapaxes(hankel, 1, 2)
-
-
-def filter_tables(rate, residue, block_len):
-    mode_weight = residue * jnp.sqrt(-jnp.expm1(-2.0 * rate))
-    offsets = lax.iota(jnp.int32, block_len)
-    lag_float = offsets.astype(jnp.float32)
-    powers = jnp.exp(-rate[None, :, :] * lag_float[:, None, None])
-    kernel = jnp.einsum("tgn,gn->gt", powers, mode_weight, precision=lax.Precision.HIGHEST)
-    toeplitz = toeplitz_from(kernel, block_len)
-    decay_into = jnp.exp(-rate[None, :, :] * (lag_float[:, None, None] + 1.0)) * mode_weight[None]
-    decay_out = jnp.exp(-rate[None, :, :] * (block_len - 1.0 - lag_float)[:, None, None])
-    block_power = jnp.exp(-rate * block_len)
-    return (toeplitz, decay_into, decay_out, block_power)
-
-
-def causal_conv(signal, tables, state_start):
-    toeplitz, decay_into, decay_out, block_power = tables
-    block_len = toeplitz.shape[1]
-    row_count, group_count, group_width = signal.shape
-    segments = signal.reshape(row_count // block_len, block_len, group_count, group_width)
-
-    def advance(state_in, segment):
-        within = jnp.einsum("gts,sgi->tgi", toeplitz, segment, precision=lax.Precision.HIGHEST)
-        carried = jnp.einsum("tgn,gni->tgi", decay_into, state_in, precision=lax.Precision.HIGHEST)
-        state_next = block_power[:, :, None] * state_in + jnp.einsum(
-            "tgn,tgi->gni", decay_out, segment, precision=lax.Precision.HIGHEST
-        )
-        return (state_next, within + carried)
-
-    state_end, outputs = lax.scan(advance, state_start, segments)
-    return (outputs.reshape(row_count, group_count, group_width), state_end)
+        compiler_params=pltpu.CompilerParams(
+            collective_id=1, has_side_effects=True, vmem_limit_bytes=48 * 1024 * 1024
+        ),
+    )(projected, short_filter, rows, down)
 
 
 def tile_count(chips):
@@ -328,33 +487,7 @@
 
 
 def local(projected, short_filter, residue, rate, out_weight):
-    row_count = projected.shape[1]
-    channels = projected.shape[2]
-    group_count = rate.shape[0]
-    prior_rows = passed_along(projected[:, -2:, :], "seq", 1)
-    extended = jnp.concatenate([prior_rows, projected], axis=1).astype(jnp.float32)
-    featured = (
-        short_filter[:, 0, None, :] * extended[:, 2:]
-        + short_filter[:, 1, None, :] * extended[:, 1 : row_count + 1]
-        + short_filter[:, 2, None, :] * extended[:, 0:row_count]
-    )
-    signal = (featured[1] * featured[2]).reshape(row_count, group_count, GROUP)
-    tables = filter_tables(rate, residue, min(256, row_count))
-    local_conv, local_end = causal_conv(
-        signal, tables, jnp.zeros((group_count, MODES, GROUP), jnp.float32)
-    )
-    device_power = jnp.exp(-rate * row_count)[:, :, None]
-
-    def relay_state(rounds, received):
-        running = device_power * received + local_end
-        return passed_along(running, "seq", 1)
-
-    incoming = lax.fori_loop(0, lax.axis_size("seq") - 1, relay_state, jnp.zeros_like(local_end))
-    lag_float = lax.iota(jnp.int32, row_count).astype(jnp.float32)
-    mode_weight = residue * jnp.sqrt(-jnp.expm1(-2.0 * rate))
-    reach = jnp.exp(-rate[None, :, :] * (lag_float[:, None, None] + 1.0)) * mode_weight[None]
-    conv = local_conv + jnp.einsum("tgn,gni->tgi", reach, incoming, precision=lax.Precision.HIGHEST)
-    mixed = (featured[0] * conv.reshape(row_count, channels)).astype(jnp.bfloat16)
+    mixed = mix(projected, short_filter, residue, rate)
     return project_and_scatter(mixed, out_weight)
 
 

time: 540 us -> 175 us (0.32)
  local copies, waits for them, and re-layouts: 253 us -> 6.49 us
  matrix products: 87.5 us -> 0 us
  other arithmetic: 24.1 us -> 0.74 us
  Pallas kernels: 146 us -> 168 us
  waiting for transfers between devices: 17.5 us -> 0 us
  starting transfers between devices: 9.16 us -> 0 us
    dynamic_update_slice x8 -> x0, local copies, waits for them, and re-layouts: 95 us -> none  [causal_conv(): state_end, outputs = lax.scan(advance, state_start, segments)]
    dot_general x14 -> x0, matrix products: 87.5 us -> none  [the longest x4 68.6 us: advance(): jnp.einsum('gts,sgi->tgi', toeplitz, segment, precision=lax.Precision.HIG...]
    reshape x3 -> x0, local copies, waits for them, and re-layouts: 45.9 us -> none  [the longest x1 34.5 us: toeplitz_from(): tiled[:, :block_len * width].reshape(group_count, block_len, width)]
    unnamed x9 -> x6, local copies, waits for them, and re-layouts: 43.6 us -> 5.99 us
    slice x3 -> x0, local copies, waits for them, and re-layouts: 24.3 us -> none  [the longest x1 22.5 us: toeplitz_from(): tiled[:, :block_len * width].reshape(group_count, block_len, width)]
    pallas_call x0 -> x1, Pallas kernels: none -> 21.9 us  [mix(): pl.pallas_call(kernel, out_shape=jax.ShapeDtypeStruct((tokens, channels),...]
    ppermute x4 -> x0, waiting for transfers between devices: 17.5 us -> none  [passed_along(): lax.ppermute(value, axis, [(source, source + steps) for source in range(l...]
    transpose x1 -> x0, local copies, waits for them, and re-layouts: 14.5 us -> none  [toeplitz_from(): return jnp.swapaxes(hankel, 1, 2)]
  transfers between devices with their start and end apart: 4 -> 0, of which waited for: 3 -> 0; matrix products, arithmetic and copies ran while one was open for 22% -> 0% of each run, Pallas kernels for 0% -> 0%
where the time goes in v2:
time: 175 us
  Pallas kernels  168 us (96%)
  local copies, waits for them, and re-layouts  6.49 us (4%)
    pallas_call x1, Pallas kernels, project_and_scatter(): pl.pallas_call(kernel, out_shape=jax.ShapeDtypeStruct((rows, width), jnp....  146 us
    pallas_call x1, Pallas kernels, mix(): pl.pallas_call(kernel, out_shape=jax.ShapeDtypeStruct((tokens, channels),...  21.9 us
    unnamed x6, local copies, waits for them, and re-layouts  5.99 us

profile of v2, /device:TPU:20, one launch (start us, length us, event | category | flops | bytes accessed | tf_op | source)
XLA Modules:
  0.0 174.8 jit_solution(16950609496113922056)
XLA Ops:
  0.0 0.7 sqrt_multiply_fusion
  0.7 0.1 copy.9
  0.8 0.1 stack_reshape.7
  0.9 0.8 copy.8
  1.7 0.1 broadcast_in_dim.7
  1.8 0.1 stack_reshape.6
  1.9 0.2 broadcast_in_dim.8.down_ref
  2.1 0.0 copy-start.1
  2.1 0.8 copy-done.1
  2.9 21.9 %shard_map.55.mixed_ref = bf16[1024,1024]{1,0:T(8,128)(2,1)S(1)} custom-call(bf16[3,1024,1024]{2,1,0:T(8,128)(2,1)} %proj.1, f32[3,3,1024]{2,1,0:T(4,128)S(1)} %copy-done.1, f32[8,2,128]{2,1,0:T(2,128)S(1)} %pad_maximum_fusion.row_ref, f32[1024,128]{1,0:T(8,128)S(1)} %broadcast_in_dim.8.down_ref), custom_call_target="tpu_custom_call" | custom-call | tf_op jit(solution)/shard_map/pallas_call | solution.py:199
  24.8 0.0 copy-start
  24.8 1.3 copy-done
  26.1 145.6 %shard_map.56 = bf16[128,8192]{1,0:T(8,128)(2,1)} custom-call(bf16[1024,1024]{1,0:T(8,128)(2,1)} %copy-done, bf16[1024,8192]{1,0:T(8,128)(2,1)} %w_ref.1), custom_call_target="tpu_custom_call" | custom-call | flops 17179869184 | bytes 16777216 | tf_op jit(solution)/shard_map/pallas_call | solution.py:462
  171.7 3.1 %copy.14 = bf16[128,8192]{1,0:T(8,128)(2,1)} copy(bf16[128,8192]{1,0:T(8,128)(2,1)} %shard_map.56) | data formatting | bytes 4194304
  (1 shorter events, 0.0 us)
Async XLA Ops:
  2.1 0.8 copy-start.1
  24.8 1.3 copy-start

commit v3 on v1

v3 whole, which is shorter than its diff:
```python
import jax
import jax.numpy as jnp
from jax import lax
from jax.experimental import pallas as pl
from jax.experimental.pallas import tpu as pltpu
from jax.sharding import PartitionSpec as P

GROUP = 16
MODES = 16
MESH = pl.DeviceIdType.MESH
WINDOW = 32
LANES = 128


def split(value):
    high = value.astype(jnp.bfloat16)
    return high, (value - high.astype(jnp.float32)).astype(jnp.bfloat16)


def iota(shape, dim):
    return lax.broadcasted_iota(jnp.int32, shape, dim)


def local(projected, short_filter, residue, rate, out_weight):
    tokens, depth = projected.shape[1:]
    width = out_weight.shape[1]
    blocks = depth // LANES
    held = LANES // GROUP
    count = lax.axis_size("seq")
    ranks = lax.axis_size("tp")
    chips = ranks // 2
    rows = tokens // ranks
    chunk = 2 * rows
    tiles = max(1, 32 // chips)
    cols = width // tiles
    piece = min(256, cols)
    lag = 2
    slots = (chips - 1) * tiles
    mode_weight = residue * jnp.sqrt(-jnp.expm1(-2.0 * rate))
    row_form = jnp.stack([rate.reshape(blocks, LANES), mode_weight.reshape(blocks, LANES)], axis=1)
    column_form = jnp.broadcast_to(rate.reshape(depth, 1), (depth, LANES))

    def kernel(proj, taps, row_ref, down_ref, w_ref, out_ref,
               proj_buf, halo, ext, table, q_buf, x_buf, s_buf, y_buf, end, landed, mixed_ref,
               w_buf, acc, stage, sib, inc, carry,
               proj_sem, halo_send, halo_recv, end_send, end_recv,
               w_sem, sib_send, sib_recv, fwd_send, in_recv, out_sem):
        me = lax.axis_index("seq")
        rank = lax.axis_index("tp")
        z = lax.div(rank, 2)
        core = lax.rem(rank, 2)
        partner = z * 2 + (1 - core)
        above = rank + 2
        below = rank - 2

        def proj_copy(b):
            slot = lax.rem(b, 2)
            return pltpu.make_async_copy(
                proj.at[:, :, pl.ds(pl.multiple_of(b * LANES, LANES), LANES)],
                proj_buf.at[slot], proj_sem.at[slot],
            )

        proj_copy(0).start()
        proj_copy(1).start()

        def w_copy(i):
            return pltpu.make_async_copy(
                w_ref.at[:, pl.ds(pl.multiple_of(i * cols, cols), cols)], w_buf.at[i], w_sem.at[i]
            )

        barrier = pltpu.get_barrier_semaphore()

        @pl.loop(1, count)
        def _(k):
            pl.semaphore_signal(
                barrier, inc=1, device_id={"seq": lax.rem(me + k, count)}, device_id_type=MESH
            )

        pl.semaphore_signal(barrier, inc=1, device_id={"tp": partner}, device_id_type=MESH)

        @pl.when(z < chips - 1)
        def _():
            pl.semaphore_signal(barrier, inc=1, device_id={"tp": above}, device_id_type=MESH)

        @pl.when(z > 0)
        def _():
            pl.semaphore_signal(barrier, inc=1, device_id={"tp": below}, device_id_type=MESH)

        middle = jnp.logical_and(z > 0, z < chips - 1)

        @pl.when(middle)
        def _():
            pl.semaphore_wait(barrier, count + 2)

        @pl.when(jnp.logical_not(middle))
        def _():
            pl.semaphore_wait(barrier, count + 1)

        def halo_copy(target):
            return pltpu.make_async_remote_copy(
                src_ref=proj.at[:, pl.ds(tokens - 16, 16), :], dst_ref=halo,
                send_sem=halo_send, recv_sem=halo_recv,
                device_id={"seq": target}, device_id_type=MESH,
            )

        def end_copy(slot, k, target):
            return pltpu.make_async_remote_copy(
                src_ref=end, dst_ref=landed.at[slot],
                send_sem=end_send.at[k], recv_sem=end_recv.at[slot],
                device_id={"seq": target}, device_id_type=MESH,
            )

        @pl.when(me < count - 1)
        def _():
            halo_copy(me + 1).start()

        @pl.loop(0, blocks)
        def _(b):
            rate_row = row_ref[b, 0:1, :]
            weight_row = row_ref[b, 1:2, :]
            lag = iota((chunk, LANES), 0).astype(jnp.float32) - (WINDOW - 1.0)
            p_high, p_low = split(jnp.exp(-rate_row * lag) * weight_row)
            rate_down = down_ref[pl.ds(pl.multiple_of(b * LANES, LANES), LANES), :]
            rate_down = jnp.concatenate([rate_down] * (held * WINDOW // LANES), axis=1)
            shape = (LANES, held * WINDOW)
            place = lax.rem(iota(shape, 1), WINDOW).astype(jnp.float32) - (WINDOW - 1.0)
            same = lax.div(iota(shape, 0), MODES) == lax.div(iota(shape, 1), WINDOW)
            g_high, g_low = split(jnp.where(same, jnp.exp(rate_down * place), 0.0))
            filled = jnp.dot(
                jnp.concatenate([p_high, p_high, p_low], axis=1),
                jnp.concatenate([g_high, g_low, g_high], axis=0),
                preferred_element_type=jnp.float32,
            )
            shape = (chunk, held * WINDOW)
            causal = iota(shape, 0) >= lax.rem(iota(shape, 1), WINDOW)
            table[b] = jnp.where(causal, filled, 0.0).astype(jnp.bfloat16)

        @pl.loop(0, tiles)
        def _(i):
            w_copy(i).start()

        @pl.when(me > 0)
        def _():
            halo_copy(me).wait_recv()

        @pl.when(me == 0)
        def _():
            halo[...] = jnp.zeros_like(halo)

        @pl.loop(0, blocks)
        def _(b):
            at = pl.ds(pl.multiple_of(b * LANES, LANES), LANES)
            slot = lax.rem(b, 2)
            proj_copy(b).wait()
            for p in range(3):
                ext[p, 0:16, :] = halo[p, :, at].astype(jnp.float32)
                ext[p, 16 : 16 + tokens, :] = proj_buf[slot, p].astype(jnp.float32)

            @pl.when(b + 2 < blocks)
            def _():
                proj_copy(b + 2).start()

            rate_down = down_ref[at, :]
            left = (chunk - 1.0) - iota((LANES, chunk), 1).astype(jnp.float32)
            if chunk > LANES:
                rate_wide = jnp.concatenate([rate_down] * (chunk // LANES), axis=1)
            else:
                rate_wide = rate_down[:, :chunk]
            e_high, e_low = split(jnp.exp(-rate_wide * left))
            decay_out = jnp.concatenate([e_high, e_low], axis=0)
            power = jnp.exp(-rate_down * float(chunk))
            shape = (LANES, LANES)
            same = lax.div(iota(shape, 0), MODES) == lax.div(iota(shape, 1), GROUP)
            running = None
            for c in range(chips):
                features = []
                for p in range(3):
                    total = None
                    for j in range(3):
                        term = taps[p, j : j + 1, at] * ext[p, pl.ds(16 - j + c * chunk, chunk), :]
                        total = term if total is None else total + term
                    features.append(total)
                q_buf[b, c] = features[0]
                signal = (features[1] * features[2]).astype(jnp.bfloat16)
                x_buf[b, c] = signal
                both = jnp.dot(decay_out, signal, preferred_element_type=jnp.float32)
                gained = jnp.where(same, both[:LANES] + both[LANES:], 0.0)
                s_buf[b, c] = gained
                running = gained if running is None else power * running + gained
            packed = running[0:MODES]
            for g in range(1, held):
                packed = packed + running[g * MODES : (g + 1) * MODES]
            end[b] = packed

        @pl.loop(1, count)
        def _(k):
            @pl.when(me + k < count)
            def _():
                end_copy(me, k, me + k).start()

        def settle_states():
            @pl.loop(0, count - 1)
            def _(source):
                @pl.when(source < me)
                def _():
                    end_copy(source, 1, me).wait_recv()

            @pl.loop(0, blocks)
            def _(b):
                rate_down = down_ref[pl.ds(pl.multiple_of(b * LANES, LANES), LANES), :]
                shape = (LANES, LANES)
                same = lax.div(iota(shape, 0), MODES) == lax.div(iota(shape, 1), GROUP)
                whole = jnp.exp(-rate_down * float(tokens))
                power = jnp.exp(-rate_down * float(chunk))
                carry[b] = jnp.zeros(shape, jnp.float32)

                @pl.loop(0, count - 1)
                def _(source):
                    @pl.when(source < me)
                    def _():
                        arrived = jnp.where(same, jnp.concatenate([landed[source, b]] * held, axis=0), 0.0)
                        carry[b] = whole * carry[b] + arrived

                running = carry[b]
                for c in range(chips):
                    gained = s_buf[b, c]
                    s_buf[b, c] = running
                    running = power * running + gained

        def finish(dest, at_first):
            @pl.loop(0, blocks)
            def _(b):
                lane = lax.div(iota((WINDOW, LANES), 1), GROUP)
                y_buf[b] = jnp.zeros((chunk, LANES), jnp.float32)
                for w in range(chunk // WINDOW):
                    begin = w * WINDOW
                    part = x_buf[b, dest, begin : begin + WINDOW, :].astype(jnp.float32)
                    spread = jnp.concatenate(
                        [jnp.where(lane == g, part, 0.0).astype(jnp.bfloat16) for g in range(held)], axis=0
                    )
                    y_buf[b, begin:chunk, :] += jnp.dot(
                        table[b, 0 : chunk - begin, :], spread, preferred_element_type=jnp.float32
                    )

            @pl.when(at_first)
            def _():
                settle_states()

            @pl.loop(0, blocks)
            def _(b):
                at = pl.ds(pl.multiple_of(b * LANES, LANES), LANES)
                s_high, s_low = split(s_buf[b, dest])
                since = iota((chunk, LANES), 0).astype(jnp.float32) + 1.0
                d_high, d_low = split(jnp.exp(-row_ref[b, 0:1, :] * since) * row_ref[b, 1:2, :])
                carried = jnp.dot(
                    jnp.concatenate([d_high, d_high, d_low], axis=1),
                    jnp.concatenate([s_high, s_low, s_high], axis=0),
                    preferred_element_type=jnp.float32,
                )
                mixed = (q_buf[b, dest] * (y_buf[b] + carried)).astype(jnp.bfloat16)
                mixed_ref[pl.ds(pl.multiple_of(dest * chunk, chunk), chunk), at] = mixed

        def sib_copy(dest, i, lane=0, turn=0):
            return pltpu.make_async_remote_copy(
                src_ref=stage.at[lane, turn], dst_ref=sib.at[dest, i],
                send_sem=sib_send.at[lane, turn], recv_sem=sib_recv.at[dest, i],
                device_id={"tp": partner}, device_id_type=MESH,
            )

        def fwd_copy(dest, i, landing, target):
            return pltpu.make_async_remote_copy(
                src_ref=acc.at[dest, i], dst_ref=inc.at[landing, i],
                send_sem=fwd_send.at[dest, i], recv_sem=in_recv.at[landing, i],
                device_id={"tp": target}, device_id_type=MESH,
            )

        def compute(dest, i, lane, k):
            turn = lax.rem(k, 2)

            @pl.when(k >= 2)
            def _():
                sib_copy(dest, i, lane, turn).wait_send()

            base = dest * (2 * rows)
            own = mixed_ref[pl.ds(pl.multiple_of(base + core * rows, rows), rows), :]
            other = mixed_ref[pl.ds(pl.multiple_of(base + (1 - core) * rows, rows), rows), :]
            left = jnp.concatenate([own, other], axis=0)

            @pl.loop(0, cols // piece)
            def _(p):
                at = pl.ds(pl.multiple_of(p * piece, piece), piece)
                product = jnp.dot(left, w_buf[i, :, at], preferred_element_type=jnp.float32)
                acc[dest, i, :, at] = product[:rows].astype(jnp.bfloat16)
                stage[lane, turn, :, at] = product[rows:].astype(jnp.bfloat16)

            sib_copy(dest, i, lane, turn).start()

        def add_in(dest, i, landing):
            @pl.loop(0, cols // piece)
            def _(p):
                at = pl.ds(pl.multiple_of(p * piece, piece), piece)
                total = acc[dest, i, :, at].astype(jnp.float32) + inc[landing, i, :, at].astype(jnp.float32)
                acc[dest, i, :, at] = (total + sib[dest, i, :, at].astype(jnp.float32)).astype(jnp.bfloat16)

        def add_sib(dest, i):
            @pl.loop(0, cols // piece)
            def _(p):
                at = pl.ds(pl.multiple_of(p * piece, piece), piece)
                total = acc[dest, i, :, at].astype(jnp.float32) + sib[dest, i, :, at].astype(jnp.float32)
                acc[dest, i, :, at] = total.astype(jnp.bfloat16)

        def up_place(k):
            return chips - 1 - lax.div(k, tiles), lax.rem(k, tiles)

        def down_place(k):
            return lax.div(k, tiles), lax.rem(k, tiles)

        up_count = (chips - 1 - z) * tiles
        down_count = z * tiles
        up_shift = z * lag
        down_shift = (chips - 1 - z) * lag
        up_first = jnp.where(z < chips - 1, up_shift, slots + lag * chips)
        down_first = jnp.where(z > 0, down_shift, slots + lag * chips)
        first = jnp.minimum(up_first, down_first)

        def forward(k, place, fed, landing_of, target):
            dest, i = place(k)

            @pl.when(k >= 2)
            def _():
                before, j = place(k - 2)
                fwd_copy(before, j, landing_of(before), target).wait_send()

            sib_copy(dest, i).wait_recv()

            @pl.when(fed)
            def _():
                fwd_copy(dest, i, dest, target).wait_recv()
                add_in(dest, i, dest)

            @pl.when(jnp.logical_not(fed))
            def _():
                add_sib(dest, i)

            fwd_copy(dest, i, landing_of(dest), target).start()

        def up_landing(dest):
            return dest

        def down_landing(dest):
            return jnp.where(dest == z - 1, chips, dest)

        @pl.loop(0, slots + 1)
        def _(it):
            w_at = it - first

            @pl.when(jnp.logical_and(w_at >= 0, w_at < tiles))
            def _():
                w_copy(w_at).wait()

            @pl.loop(0, chips)
            def _(dest):
                needed = jnp.where(dest > z, up_shift + (chips - 1 - dest) * tiles, down_shift + dest * tiles)
                needed = jnp.where(dest == z, first + tiles, needed)

                @pl.when(it == needed)
                def _():
                    finish(dest, it == first)

            ku = it - up_shift

            @pl.when(jnp.logical_and(ku >= 0, ku < up_count))
            def _():
                dest, i = up_place(ku)
                compute(dest, i, 0, ku)

            kd = it - down_shift

            @pl.when(jnp.logical_and(kd >= 0, kd < down_count))
            def _():
                dest, i = down_place(kd)
                compute(dest, i, 1, kd)

            ks = it - first - tiles

            @pl.when(jnp.logical_and(ks >= 0, ks < tiles))
            def _():
                compute(z, ks, 2, ks)

            @pl.when(jnp.logical_and(ku >= 1, ku <= up_count))
            def _():
                forward(ku - 1, up_place, z > 0, up_landing, above)

            @pl.when(jnp.logical_and(kd >= 1, kd <= down_count))
            def _():
                forward(kd - 1, down_place, z < chips - 1, down_landing, below)

        def drain(count, place, landing_of, target):
            @pl.when(count >= 2)
            def _():
                for back in (2, 1):
                    dest, i = place(count - back)
                    fwd_copy(dest, i, landing_of(dest), target).wait_send()

            @pl.when(count == 1)
            def _():
                dest, i = place(count - 1)
                fwd_copy(dest, i, landing_of(dest), target).wait_send()

        def out_copy(i):
            return pltpu.make_async_copy(
                acc.at[z, i], out_ref.at[:, pl.ds(pl.multiple_of(i * cols, cols), cols)], out_sem.at[i]
            )

        @pl.loop(0, tiles)
        def _(i):
            sib_copy(z, i).wait_recv()

            @pl.when(z < chips - 1)
            def _():
                fwd_copy(z, i, chips, above).wait_recv()

            @pl.when(z > 0)
            def _():
                fwd_copy(z, i, z, below).wait_recv()

            @pl.when(z == 0)
            def _():
                add_in(z, i, chips)

            @pl.when(z == chips - 1)
            def _():
                add_in(z, i, z)

            @pl.when(middle)
            def _():
                @pl.loop(0, cols // piece)
                def _(p):
                    at = pl.ds(pl.multiple_of(p * piece, piece), piece)
                    total = acc[z, i, :, at].astype(jnp.float32) + sib[z, i, :, at].astype(jnp.float32)
                    total = total + inc[z, i, :, at].astype(jnp.float32)
                    total = total + inc[chips, i, :, at].astype(jnp.float32)
                    acc[z, i, :, at] = total.astype(jnp.bfloat16)

            out_copy(i).start()

        drain(up_count, up_place, up_landing, above)
        drain(down_count, down_place, down_landing, below)

        @pl.loop(0, tiles)
        def _(i):
            out_copy(i).wait()

        for turn in range(2):
            sib_copy(z, 0, 2, turn).wait_send()

            @pl.when(up_count > 0)
            def _():
                sib_copy(z, 0, 0, turn).wait_send()

            @pl.when(down_count > 0)
            def _():
                sib_copy(z, 0, 1, turn).wait_send()

        @pl.when(me < count - 1)
        def _():
            halo_copy(me + 1).wait_send()

        @pl.loop(1, count)
        def _(k):
            @pl.when(me + k < count)
            def _():
                end_copy(me, k, me + k).wait_send()

    block = (chips, tiles, rows, cols)
    inside = pl.BlockSpec(memory_space=pltpu.VMEM)
    outside = pl.BlockSpec(memory_space=pl.ANY)
    return pl.pallas_call(
        kernel,
        out_shape=jax.ShapeDtypeStruct((rows, width), jnp.bfloat16),
        in_specs=[outside, inside, inside, inside, outside],
        out_specs=outside,
        scratch_shapes=[
            pltpu.VMEM((2, 3, tokens, LANES), jnp.bfloat16),
            pltpu.VMEM((3, 16, depth), jnp.bfloat16),
            pltpu.VMEM((3, 16 + tokens, LANES), jnp.float32),
            pltpu.VMEM((blocks, chunk, held * WINDOW), jnp.bfloat16),
            pltpu.VMEM((blocks, chips, chunk, LANES), jnp.float32),
            pltpu.VMEM((blocks, chips, chunk, LANES), jnp.bfloat16),
            pltpu.VMEM((blocks, chips, LANES, LANES), jnp.float32),
            pltpu.VMEM((blocks, chunk, LANES), jnp.float32),
            pltpu.VMEM((blocks, MODES, LANES), jnp.float32),
            pltpu.VMEM((count, blocks, MODES, LANES), jnp.float32),
            pltpu.VMEM((tokens, depth), jnp.bfloat16),
            pltpu.VMEM((tiles, depth, cols), jnp.bfloat16),
            pltpu.VMEM(block, jnp.bfloat16),
            pltpu.VMEM((3, 2, rows, cols), jnp.bfloat16),
            pltpu.VMEM(block, jnp.bfloat16),
            pltpu.VMEM((chips + 1, tiles, rows, cols), jnp.bfloat16),
            pltpu.VMEM((blocks, LANES, LANES), jnp.float32),
            pltpu.SemaphoreType.DMA((2,)),
            pltpu.SemaphoreType.DMA,
            pltpu.SemaphoreType.DMA,
            pltpu.SemaphoreType.DMA((count,)),
            pltpu.SemaphoreType.DMA((count,)),
            pltpu.SemaphoreType.DMA((tiles,)),
            pltpu.SemaphoreType.DMA((3, 2)),
            pltpu.SemaphoreType.DMA((chips, tiles)),
            pltpu.SemaphoreType.DMA((chips, tiles)),
            pltpu.SemaphoreType.DMA((chips + 1, tiles)),
            pltpu.SemaphoreType.DMA((tiles,)),
        ],
        compiler_params=pltpu.CompilerParams(
            collective_id=0, has_side_effects=True, vmem_limit_bytes=63 * 1024 * 1024
        ),
    )(projected, short_filter, row_form, column_form, out_weight)


def solution(mesh):
    placed = (
        P(None, "seq", "tp"),
        P(None, None, "tp"),
        P("tp", None),
        P("tp", None),
        P("tp", None),
    )
    return jax.shard_map(
        local, mesh=mesh, in_specs=placed, out_specs=P(("seq", "tp"), None), check_vma=False
    )
```

time: 540 us -> 172 us (0.32)
  local copies, waits for them, and re-layouts: 253 us -> 5.19 us
  matrix products: 87.5 us -> 0 us
  other arithmetic: 24.1 us -> 1.34 us
  Pallas kernels: 146 us -> 165 us
  waiting for transfers between devices: 17.5 us -> 0 us
  starting transfers between devices: 9.16 us -> 0 us
    dynamic_update_slice x8 -> x0, local copies, waits for them, and re-layouts: 95 us -> none  [causal_conv(): state_end, outputs = lax.scan(advance, state_start, segments)]
    dot_general x14 -> x0, matrix products: 87.5 us -> none  [the longest x4 68.6 us: advance(): jnp.einsum('gts,sgi->tgi', toeplitz, segment, precision=lax.Precision.HIG...]
    reshape x3 -> x0, local copies, waits for them, and re-layouts: 45.9 us -> none  [the longest x1 34.5 us: toeplitz_from(): tiled[:, :block_len * width].reshape(group_count, block_len, width)]
    unnamed x9 -> x2, local copies, waits for them, and re-layouts: 43.6 us -> 3.88 us
    slice x3 -> x0, local copies, waits for them, and re-layouts: 24.3 us -> none  [the longest x1 22.5 us: toeplitz_from(): tiled[:, :block_len * width].reshape(group_count, block_len, width)]
    pallas_call x1, Pallas kernels: 146 us -> 165 us  [local(): pl.pallas_call(kernel, out_shape=jax.ShapeDtypeStruct((rows, width), jnp....]
    ppermute x4 -> x0, waiting for transfers between devices: 17.5 us -> none  [passed_along(): lax.ppermute(value, axis, [(source, source + steps) for source in range(l...]
    transpose x1 -> x0, local copies, waits for them, and re-layouts: 14.5 us -> none  [toeplitz_from(): return jnp.swapaxes(hankel, 1, 2)]
  transfers between devices with their start and end apart: 4 -> 0, of which waited for: 3 -> 0; matrix products, arithmetic and copies ran while one was open for 22% -> 0% of each run, Pallas kernels for 0% -> 0%
where the time goes in v3:
time: 172 us
  Pallas kernels  165 us (96%)
  local copies, waits for them, and re-layouts  5.19 us (3%)
    pallas_call x1, Pallas kernels, local(): pl.pallas_call(kernel, out_shape=jax.ShapeDtypeStruct((rows, width), jnp....  165 us
    unnamed x2, local copies, waits for them, and re-layouts  3.88 us

profile of v3, /device:TPU:20, one launch (start us, length us, event | category | flops | bytes accessed | tf_op | source)
XLA Modules:
  0.0 171.6 jit_solution(18164902586667012446)
XLA Ops:
  0.0 0.7 sqrt_multiply_fusion
  0.7 0.1 copy.9
  0.8 0.1 stack_reshape.7
  0.9 0.8 copy.8
  1.7 0.1 broadcast_in_dim.7
  1.8 0.1 stack_reshape.6
  1.8 0.6 pad_maximum_fusion.row_ref
  2.4 1.0 broadcast_in_dim.8.down_ref
  3.4 165.1 %shard_map.55 = bf16[128,8192]{1,0:T(8,128)(2,1)} custom-call(bf16[3,1024,1024]{2,1,0:T(8,128)(2,1)} %proj.1, f32[3,3,1024]{2,1,0:T(4,128)} %taps.1, f32[8,2,128]{2,1,0:T(2,128)} %pad_maximum_fusion.row_ref, f32[1024,128]{1,0:T(8,128)} %broadcast_in_dim.8.down_ref, bf16[1024,8192]{1,0:T(8,128)(2,1)} %w_ref.1), custom_call_target="tpu_custom_call" | custom-call | tf_op jit(solution)/shard_map/pallas_call | solution.py:478
  168.5 3.1 %copy.14 = bf16[128,8192]{1,0:T(8,128)(2,1)} copy(bf16[128,8192]{1,0:T(8,128)(2,1)} %shard_map.55) | data formatting | bytes 4194304

commit v4 on v3

--- a/solution.py
+++ b/solution.py
@@ -35,13 +35,12 @@
     cols = width // tiles
     piece = min(256, cols)
     lag = 2
+    flying = 3
     slots = (chips - 1) * tiles
     mode_weight = residue * jnp.sqrt(-jnp.expm1(-2.0 * rate))
-    row_form = jnp.stack([rate.reshape(blocks, LANES), mode_weight.reshape(blocks, LANES)], axis=1)
-    column_form = jnp.broadcast_to(rate.reshape(depth, 1), (depth, LANES))
-
-    def kernel(proj, taps, row_ref, down_ref, w_ref, out_ref,
-               proj_buf, halo, ext, table, q_buf, x_buf, s_buf, y_buf, end, landed, mixed_ref,
+
+    def kernel(proj, taps, rate_ref, weight_ref, w_ref, out_ref,
+               proj_buf, halo, ext, q_ext, down_ref, table, q_buf, x_buf, s_buf, y_buf, end, landed, mixed_ref,
                w_buf, acc, stage, sib, inc, carry,
                proj_sem, halo_send, halo_recv, end_send, end_recv,
                w_sem, sib_send, sib_recv, fwd_send, in_recv, out_sem):
@@ -116,12 +115,12 @@
 
         @pl.loop(0, blocks)
         def _(b):
-            rate_row = row_ref[b, 0:1, :]
-            weight_row = row_ref[b, 1:2, :]
+            rate_row = rate_ref[pl.ds(b, 1), :]
+            weight_row = weight_ref[pl.ds(b, 1), :]
+            down_ref[b] = jnp.broadcast_to(rate_row, (LANES, LANES)).T
             lag = iota((chunk, LANES), 0).astype(jnp.float32) - (WINDOW - 1.0)
             p_high, p_low = split(jnp.exp(-rate_row * lag) * weight_row)
-            rate_down = down_ref[pl.ds(pl.multiple_of(b * LANES, LANES), LANES), :]
-            rate_down = jnp.concatenate([rate_down] * (held * WINDOW // LANES), axis=1)
+            rate_down = jnp.concatenate([down_ref[b]] * (held * WINDOW // LANES), axis=1)
             shape = (LANES, held * WINDOW)
             place = lax.rem(iota(shape, 1), WINDOW).astype(jnp.float32) - (WINDOW - 1.0)
             same = lax.div(iota(shape, 0), MODES) == lax.div(iota(shape, 1), WINDOW)
@@ -152,15 +151,17 @@
             at = pl.ds(pl.multiple_of(b * LANES, LANES), LANES)
             slot = lax.rem(b, 2)
             proj_copy(b).wait()
-            for p in range(3):
-                ext[p, 0:16, :] = halo[p, :, at].astype(jnp.float32)
-                ext[p, 16 : 16 + tokens, :] = proj_buf[slot, p].astype(jnp.float32)
+            q_buf[b, 0:16, :] = halo[0, :, at]
+            q_buf[b, 16 : 16 + tokens, :] = proj_buf[slot, 0]
+            for p in (1, 2):
+                ext[p - 1, 0:16, :] = halo[p, :, at].astype(jnp.float32)
+                ext[p - 1, 16 : 16 + tokens, :] = proj_buf[slot, p].astype(jnp.float32)
 
             @pl.when(b + 2 < blocks)
             def _():
                 proj_copy(b + 2).start()
 
-            rate_down = down_ref[at, :]
+            rate_down = down_ref[b]
             left = (chunk - 1.0) - iota((LANES, chunk), 1).astype(jnp.float32)
             if chunk > LANES:
                 rate_wide = jnp.concatenate([rate_down] * (chunk // LANES), axis=1)
@@ -174,14 +175,13 @@
             running = None
             for c in range(chips):
                 features = []
-                for p in range(3):
+                for p in (1, 2):
                     total = None
                     for j in range(3):
-                        term = taps[p, j : j + 1, at] * ext[p, pl.ds(16 - j + c * chunk, chunk), :]
+                        term = taps[p, j : j + 1, at] * ext[p - 1, pl.ds(16 - j + c * chunk, chunk), :]
                         total = term if total is None else total + term
                     features.append(total)
-                q_buf[b, c] = features[0]
-                signal = (features[1] * features[2]).astype(jnp.bfloat16)
+                signal = (features[0] * features[1]).astype(jnp.bfloat16)
                 x_buf[b, c] = signal
                 both = jnp.dot(decay_out, signal, preferred_element_type=jnp.float32)
                 gained = jnp.where(same, both[:LANES] + both[LANES:], 0.0)
@@ -207,7 +207,7 @@
 
             @pl.loop(0, blocks)
             def _(b):
-                rate_down = down_ref[pl.ds(pl.multiple_of(b * LANES, LANES), LANES), :]
+                rate_down = down_ref[b]
                 shape = (LANES, LANES)
                 same = lax.div(iota(shape, 0), MODES) == lax.div(iota(shape, 1), GROUP)
                 whole = jnp.exp(-rate_down * float(tokens))
@@ -227,38 +227,36 @@
                     s_buf[b, c] = running
                     running = power * running + gained
 
-        def finish(dest, at_first):
-            @pl.loop(0, blocks)
-            def _(b):
-                lane = lax.div(iota((WINDOW, LANES), 1), GROUP)
-                y_buf[b] = jnp.zeros((chunk, LANES), jnp.float32)
-                for w in range(chunk // WINDOW):
-                    begin = w * WINDOW
-                    part = x_buf[b, dest, begin : begin + WINDOW, :].astype(jnp.float32)
-                    spread = jnp.concatenate(
-                        [jnp.where(lane == g, part, 0.0).astype(jnp.bfloat16) for g in range(held)], axis=0
-                    )
-                    y_buf[b, begin:chunk, :] += jnp.dot(
-                        table[b, 0 : chunk - begin, :], spread, preferred_element_type=jnp.float32
-                    )
-
-            @pl.when(at_first)
-            def _():
-                settle_states()
-
-            @pl.loop(0, blocks)
-            def _(b):
-                at = pl.ds(pl.multiple_of(b * LANES, LANES), LANES)
-                s_high, s_low = split(s_buf[b, dest])
-                since = iota((chunk, LANES), 0).astype(jnp.float32) + 1.0
-                d_high, d_low = split(jnp.exp(-row_ref[b, 0:1, :] * since) * row_ref[b, 1:2, :])
-                carried = jnp.dot(
-                    jnp.concatenate([d_high, d_high, d_low], axis=1),
-                    jnp.concatenate([s_high, s_low, s_high], axis=0),
-                    preferred_element_type=jnp.float32,
+        def convolve(dest, b):
+            lane = lax.div(iota((WINDOW, LANES), 1), GROUP)
+            y_buf[b] = jnp.zeros((chunk, LANES), jnp.float32)
+            for w in range(chunk // WINDOW):
+                begin = w * WINDOW
+                part = x_buf[b, dest, begin : begin + WINDOW, :].astype(jnp.float32)
+                spread = jnp.concatenate(
+                    [jnp.where(lane == g, part, 0.0).astype(jnp.bfloat16) for g in range(held)], axis=0
                 )
-                mixed = (q_buf[b, dest] * (y_buf[b] + carried)).astype(jnp.bfloat16)
-                mixed_ref[pl.ds(pl.multiple_of(dest * chunk, chunk), chunk), at] = mixed
+                y_buf[b, begin:chunk, :] += jnp.dot(
+                    table[b, 0 : chunk - begin, :], spread, preferred_element_type=jnp.float32
+                )
+
+        def combine(dest, b):
+            at = pl.ds(pl.multiple_of(b * LANES, LANES), LANES)
+            start = pl.multiple_of(dest * chunk, chunk)
+            q_ext[...] = q_buf[b, pl.ds(start, chunk + 16), :].astype(jnp.float32)
+            query = None
+            for j in range(3):
+                term = taps[0, j : j + 1, at] * q_ext[16 - j : 16 - j + chunk, :]
+                query = term if query is None else query + term
+            s_high, s_low = split(s_buf[b, dest])
+            since = iota((chunk, LANES), 0).astype(jnp.float32) + 1.0
+            d_high, d_low = split(jnp.exp(-rate_ref[pl.ds(b, 1), :] * since) * weight_ref[pl.ds(b, 1), :])
+            carried = jnp.dot(
+                jnp.concatenate([d_high, d_high, d_low], axis=1),
+                jnp.concatenate([s_high, s_low, s_high], axis=0),
+                preferred_element_type=jnp.float32,
+            )
+            mixed_ref[pl.ds(start, chunk), at] = (query * (y_buf[b] + carried)).astype(jnp.bfloat16)
 
         def sib_copy(dest, i, lane=0, turn=0):
             return pltpu.make_async_remote_copy(
@@ -322,13 +320,15 @@
         up_first = jnp.where(z < chips - 1, up_shift, slots + lag * chips)
         down_first = jnp.where(z > 0, down_shift, slots + lag * chips)
         first = jnp.minimum(up_first, down_first)
+        self_first = first + tiles + tiles // 2
+        share = -(-blocks // tiles)
 
         def forward(k, place, fed, landing_of, target):
             dest, i = place(k)
 
-            @pl.when(k >= 2)
-            def _():
-                before, j = place(k - 2)
+            @pl.when(k >= flying)
+            def _():
+                before, j = place(k - flying)
                 fwd_copy(before, j, landing_of(before), target).wait_send()
 
             sib_copy(dest, i).wait_recv()
@@ -358,14 +358,36 @@
             def _():
                 w_copy(w_at).wait()
 
+            @pl.when(it == first)
+            def _():
+                dest = jnp.where(first == up_first, chips - 1, 0)
+
+                @pl.loop(0, blocks)
+                def _(b):
+                    convolve(dest, b)
+
+                settle_states()
+
+                @pl.loop(0, blocks)
+                def _(b):
+                    combine(dest, b)
+
             @pl.loop(0, chips)
             def _(dest):
                 needed = jnp.where(dest > z, up_shift + (chips - 1 - dest) * tiles, down_shift + dest * tiles)
-                needed = jnp.where(dest == z, first + tiles, needed)
-
-                @pl.when(it == needed)
-                def _():
-                    finish(dest, it == first)
+                needed = jnp.where(dest == z, self_first, needed)
+                turn = it - needed + tiles - 1
+                gradual = needed - tiles + 1 > first
+                inside = jnp.logical_and(turn >= 0, turn < tiles)
+                low = jnp.where(gradual, turn * share, 0)
+                high = jnp.where(gradual, jnp.minimum(low + share, blocks), blocks)
+                active = jnp.logical_and(needed != first, jnp.where(gradual, inside, it == needed))
+                high = jnp.where(active, high, low)
+
+                @pl.loop(low, high)
+                def _(b):
+                    convolve(dest, b)
+                    combine(dest, b)
 
             ku = it - up_shift
 
@@ -381,7 +403,7 @@
                 dest, i = down_place(kd)
                 compute(dest, i, 1, kd)
 
-            ks = it - first - tiles
+            ks = it - self_first
 
             @pl.when(jnp.logical_and(ks >= 0, ks < tiles))
             def _():
@@ -396,16 +418,11 @@
                 forward(kd - 1, down_place, z < chips - 1, down_landing, below)
 
         def drain(count, place, landing_of, target):
-            @pl.when(count >= 2)
-            def _():
-                for back in (2, 1):
+            for back in range(flying, 0, -1):
+                @pl.when(count >= back)
+                def _():
                     dest, i = place(count - back)
                     fwd_copy(dest, i, landing_of(dest), target).wait_send()
-
-            @pl.when(count == 1)
-            def _():
-                dest, i = place(count - 1)
-                fwd_copy(dest, i, landing_of(dest), target).wait_send()
 
         def out_copy(i):
             return pltpu.make_async_copy(
@@ -483,9 +500,11 @@
         scratch_shapes=[
             pltpu.VMEM((2, 3, tokens, LANES), jnp.bfloat16),
             pltpu.VMEM((3, 16, depth), jnp.bfloat16),
-            pltpu.VMEM((3, 16 + tokens, LANES), jnp.float32),
+            pltpu.VMEM((2, 16 + tokens, LANES), jnp.float32),
+            pltpu.VMEM((16 + chunk, LANES), jnp.float32),
+            pltpu.VMEM((blocks, LANES, LANES), jnp.float32),
             pltpu.VMEM((blocks, chunk, held * WINDOW), jnp.bfloat16),
-            pltpu.VMEM((blocks, chips, chunk, LANES), jnp.float32),
+            pltpu.VMEM((blocks, 16 + tokens, LANES), jnp.bfloat16),
             pltpu.VMEM((blocks, chips, chunk, LANES), jnp.bfloat16),
             pltpu.VMEM((blocks, chips, LANES, LANES), jnp.float32),
             pltpu.VMEM((blocks, chunk, LANES), jnp.float32),
@@ -513,7 +532,9 @@
         compiler_params=pltpu.CompilerParams(
             collective_id=0, has_side_effects=True, vmem_limit_bytes=63 * 1024 * 1024
         ),
-    )(projected, short_filter, row_form, column_form, out_weight)
+    )(
+        projected, short_filter, rate.reshape(blocks, LANES), mode_weight.reshape(blocks, LANES), out_weight
+    )
 
 
 def solution(mesh):

time: 172 us -> 171 us (level)
  no operation moved by 1% of the time
where the time goes in v4:
time: 171 us
  Pallas kernels  165 us (96%)
  local copies, waits for them, and re-layouts  5.31 us (3%)
    pallas_call x1, Pallas kernels, local(): pl.pallas_call(kernel, out_shape=jax.ShapeDtypeStruct((rows, width), jnp....  165 us
    unnamed x2, local copies, waits for them, and re-layouts  3.87 us

profile of v4, /device:TPU:20, one launch (start us, length us, event | category | flops | bytes accessed | tf_op | source)
XLA Modules:
  0.0 170.9 jit_solution(13211053848355004330)
XLA Ops:
  0.0 0.7 sqrt_multiply_fusion
  0.7 0.1 copy.9
  0.8 0.7 reshape.7.weight_ref
  1.5 0.8 copy.8
  2.3 0.7 reshape.6.rate_ref
  2.9 164.9 %shard_map.55 = bf16[128,8192]{1,0:T(8,128)(2,1)} custom-call(bf16[3,1024,1024]{2,1,0:T(8,128)(2,1)} %proj.1, f32[3,3,1024]{2,1,0:T(4,128)} %taps.1, f32[8,128]{1,0:T(8,128)} %reshape.6.rate_ref, f32[8,128]{1,0:T(8,128)} %reshape.7.weight_ref, bf16[1024,8192]{1,0:T(8,128)(2,1)} %w_ref.1), custom_call_target="tpu_custom_call" | custom-call | tf_op jit(solution)/shard_map/pallas_call | solution.py:495
  167.8 3.1 %copy.11 = bf16[128,8192]{1,0:T(8,128)(2,1)} copy(bf16[128,8192]{1,0:T(8,128)(2,1)} %shard_map.55) | data formatting | bytes 4194304

commit v5 on v4

--- a/solution.py
+++ b/solution.py
@@ -19,6 +19,10 @@
 
 def iota(shape, dim):
     return lax.broadcasted_iota(jnp.int32, shape, dim)
+
+
+def group_of(shape, dim, size):
+    return lax.shift_right_logical(iota(shape, dim), size.bit_length() - 1)
 
 
 def local(projected, short_filter, residue, rate, out_weight):
@@ -113,7 +117,7 @@
         def _():
             halo_copy(me + 1).start()
 
-        @pl.loop(0, blocks)
+        @pl.loop(0, blocks, unroll=2)
         def _(b):
             rate_row = rate_ref[pl.ds(b, 1), :]
             weight_row = weight_ref[pl.ds(b, 1), :]
@@ -122,8 +126,8 @@
             p_high, p_low = split(jnp.exp(-rate_row * lag) * weight_row)
             rate_down = jnp.concatenate([down_ref[b]] * (held * WINDOW // LANES), axis=1)
             shape = (LANES, held * WINDOW)
-            place = lax.rem(iota(shape, 1), WINDOW).astype(jnp.float32) - (WINDOW - 1.0)
-            same = lax.div(iota(shape, 0), MODES) == lax.div(iota(shape, 1), WINDOW)
+            place = (iota(shape, 1) & (WINDOW - 1)).astype(jnp.float32) - (WINDOW - 1.0)
+            same = group_of(shape, 0, MODES) == group_of(shape, 1, WINDOW)
             g_high, g_low = split(jnp.where(same, jnp.exp(rate_down * place), 0.0))
             filled = jnp.dot(
                 jnp.concatenate([p_high, p_high, p_low], axis=1),
@@ -131,8 +135,9 @@
                 preferred_element_type=jnp.float32,
             )
             shape = (chunk, held * WINDOW)
-            causal = iota(shape, 0) >= lax.rem(iota(shape, 1), WINDOW)
-            table[b] = jnp.where(causal, filled, 0.0).astype(jnp.bfloat16)
+            causal = iota(shape, 0) >= (iota(shape, 1) & (WINDOW - 1))
+            table[b, 0:chunk, :] = jnp.zeros(shape, jnp.bfloat16)
+            table[b, chunk : 2 * chunk, :] = jnp.where(causal, filled, 0.0).astype(jnp.bfloat16)
 
         @pl.loop(0, tiles)
         def _(i):
@@ -171,7 +176,7 @@
             decay_out = jnp.concatenate([e_high, e_low], axis=0)
             power = jnp.exp(-rate_down * float(chunk))
             shape = (LANES, LANES)
-            same = lax.div(iota(shape, 0), MODES) == lax.div(iota(shape, 1), GROUP)
+            same = group_of(shape, 0, MODES) == group_of(shape, 1, GROUP)
             running = None
             for c in range(chips):
                 features = []
@@ -209,7 +214,7 @@
             def _(b):
                 rate_down = down_ref[b]
                 shape = (LANES, LANES)
-                same = lax.div(iota(shape, 0), MODES) == lax.div(iota(shape, 1), GROUP)
+                same = group_of(shape, 0, MODES) == group_of(shape, 1, GROUP)
                 whole = jnp.exp(-rate_down * float(tokens))
                 power = jnp.exp(-rate_down * float(chunk))
                 carry[b] = jnp.zeros(shape, jnp.float32)
@@ -228,17 +233,18 @@
                     running = power * running + gained
 
         def convolve(dest, b):
-            lane = lax.div(iota((WINDOW, LANES), 1), GROUP)
-            y_buf[b] = jnp.zeros((chunk, LANES), jnp.float32)
+            lane = group_of((WINDOW, LANES), 1, GROUP)
+            shifted, spread = [], []
             for w in range(chunk // WINDOW):
                 begin = w * WINDOW
                 part = x_buf[b, dest, begin : begin + WINDOW, :].astype(jnp.float32)
-                spread = jnp.concatenate(
-                    [jnp.where(lane == g, part, 0.0).astype(jnp.bfloat16) for g in range(held)], axis=0
-                )
-                y_buf[b, begin:chunk, :] += jnp.dot(
-                    table[b, 0 : chunk - begin, :], spread, preferred_element_type=jnp.float32
-                )
+                spread += [jnp.where(lane == g, part, 0.0).astype(jnp.bfloat16) for g in range(held)]
+                shifted.append(table[b, chunk - begin : 2 * chunk - begin, :])
+            y_buf[b] = jnp.dot(
+                jnp.concatenate(shifted, axis=1),
+                jnp.concatenate(spread, axis=0),
+                preferred_element_type=jnp.float32,
+            )
 
         def combine(dest, b):
             at = pl.ds(pl.multiple_of(b * LANES, LANES), LANES)
@@ -362,13 +368,13 @@
             def _():
                 dest = jnp.where(first == up_first, chips - 1, 0)
 
-                @pl.loop(0, blocks)
+                @pl.loop(0, blocks, unroll=2)
                 def _(b):
                     convolve(dest, b)
 
                 settle_states()
 
-                @pl.loop(0, blocks)
+                @pl.loop(0, blocks, unroll=2)
                 def _(b):
                     combine(dest, b)
 
@@ -503,7 +509,7 @@
             pltpu.VMEM((2, 16 + tokens, LANES), jnp.float32),
             pltpu.VMEM((16 + chunk, LANES), jnp.float32),
             pltpu.VMEM((blocks, LANES, LANES), jnp.float32),
-            pltpu.VMEM((blocks, chunk, held * WINDOW), jnp.bfloat16),
+            pltpu.VMEM((blocks, 2 * chunk, held * WINDOW), jnp.bfloat16),
             pltpu.VMEM((blocks, 16 + tokens, LANES), jnp.bfloat16),
             pltpu.VMEM((blocks, chips, chunk, LANES), jnp.bfloat16),
             pltpu.VMEM((blocks, chips, LANES, LANES), jnp.float32),

time: 171 us -> 170 us (level)
  no operation moved by 1% of the time
where the time goes in v5:
time: 170 us
  Pallas kernels  164 us (96%)
  local copies, waits for them, and re-layouts  5.31 us (3%)
    pallas_call x1, Pallas kernels, local(): pl.pallas_call(kernel, out_shape=jax.ShapeDtypeStruct((rows, width), jnp....  164 us
    unnamed x2, local copies, waits for them, and re-layouts  3.87 us

profile of v5, /device:TPU:20, one launch (start us, length us, event | category | flops | bytes accessed | tf_op | source)
XLA Modules:
  0.0 169.6 jit_solution(18268433714995758028)
XLA Ops:
  0.0 0.7 sqrt_multiply_fusion
  0.7 0.1 copy.9
  0.8 0.7 reshape.7.weight_ref
  1.5 0.8 copy.8
  2.3 0.7 reshape.6.rate_ref
  2.9 163.5 %shard_map.55 = bf16[128,8192]{1,0:T(8,128)(2,1)} custom-call(bf16[3,1024,1024]{2,1,0:T(8,128)(2,1)} %proj.1, f32[3,3,1024]{2,1,0:T(4,128)} %taps.1, f32[8,128]{1,0:T(8,128)} %reshape.6.rate_ref, f32[8,128]{1,0:T(8,128)} %reshape.7.weight_ref, bf16[1024,8192]{1,0:T(8,128)(2,1)} %w_ref.1), custom_call_target="tpu_custom_call" | custom-call | tf_op jit(solution)/shard_map/pallas_call | solution.py:501
  166.5 3.1 %copy.11 = bf16[128,8192]{1,0:T(8,128)(2,1)} copy(bf16[128,8192]{1,0:T(8,128)(2,1)} %shard_map.55) | data formatting | bytes 4194304

commit v6 on v5

--- a/solution.py
+++ b/solution.py
@@ -46,7 +46,7 @@
     def kernel(proj, taps, rate_ref, weight_ref, w_ref, out_ref,
                proj_buf, halo, ext, q_ext, down_ref, table, q_buf, x_buf, s_buf, y_buf, end, landed, mixed_ref,
                w_buf, acc, stage, sib, inc, carry,
-               proj_sem, halo_send, halo_recv, end_send, end_recv,
+               proj_sem, query_sem, halo_send, halo_recv, end_send, end_recv,
                w_sem, sib_send, sib_recv, fwd_send, in_recv, out_sem):
         me = lax.axis_index("seq")
         rank = lax.axis_index("tp")
@@ -57,14 +57,20 @@
         below = rank - 2
 
         def proj_copy(b):
-            slot = lax.rem(b, 2)
             return pltpu.make_async_copy(
-                proj.at[:, :, pl.ds(pl.multiple_of(b * LANES, LANES), LANES)],
-                proj_buf.at[slot], proj_sem.at[slot],
-            )
-
-        proj_copy(0).start()
-        proj_copy(1).start()
+                proj.at[pl.ds(1, 2), :, pl.ds(pl.multiple_of(b * LANES, LANES), LANES)],
+                proj_buf.at[b], proj_sem.at[b],
+            )
+
+        def query_copy(b):
+            return pltpu.make_async_copy(
+                proj.at[0, :, pl.ds(pl.multiple_of(b * LANES, LANES), LANES)],
+                q_buf.at[b, pl.ds(16, tokens), :], query_sem.at[b],
+            )
+
+        @pl.loop(0, blocks)
+        def _(b):
+            proj_copy(b).start()
 
         def w_copy(i):
             return pltpu.make_async_copy(
@@ -139,6 +145,10 @@
             table[b, 0:chunk, :] = jnp.zeros(shape, jnp.bfloat16)
             table[b, chunk : 2 * chunk, :] = jnp.where(causal, filled, 0.0).astype(jnp.bfloat16)
 
+        @pl.loop(0, blocks)
+        def _(b):
+            query_copy(b).start()
+
         @pl.loop(0, tiles)
         def _(i):
             w_copy(i).start()
@@ -154,17 +164,11 @@
         @pl.loop(0, blocks)
         def _(b):
             at = pl.ds(pl.multiple_of(b * LANES, LANES), LANES)
-            slot = lax.rem(b, 2)
             proj_copy(b).wait()
             q_buf[b, 0:16, :] = halo[0, :, at]
-            q_buf[b, 16 : 16 + tokens, :] = proj_buf[slot, 0]
             for p in (1, 2):
                 ext[p - 1, 0:16, :] = halo[p, :, at].astype(jnp.float32)
-                ext[p - 1, 16 : 16 + tokens, :] = proj_buf[slot, p].astype(jnp.float32)
-
-            @pl.when(b + 2 < blocks)
-            def _():
-                proj_copy(b + 2).start()
+                ext[p - 1, 16 : 16 + tokens, :] = proj_buf[b, p - 1].astype(jnp.float32)
 
             rate_down = down_ref[b]
             left = (chunk - 1.0) - iota((LANES, chunk), 1).astype(jnp.float32)
@@ -203,6 +207,10 @@
             def _():
                 end_copy(me, k, me + k).start()
 
+        @pl.loop(0, blocks)
+        def _(b):
+            query_copy(b).wait()
+
         def settle_states():
             @pl.loop(0, count - 1)
             def _(source):
@@ -504,7 +512,7 @@
         in_specs=[outside, inside, inside, inside, outside],
         out_specs=outside,
         scratch_shapes=[
-            pltpu.VMEM((2, 3, tokens, LANES), jnp.bfloat16),
+            pltpu.VMEM((blocks, 2, tokens, LANES), jnp.bfloat16),
             pltpu.VMEM((3, 16, depth), jnp.bfloat16),
             pltpu.VMEM((2, 16 + tokens, LANES), jnp.float32),
             pltpu.VMEM((16 + chunk, LANES), jnp.float32),
@@ -523,7 +531,8 @@
             pltpu.VMEM(block, jnp.bfloat16),
             pltpu.VMEM((chips + 1, tiles, rows, cols), jnp.bfloat16),
             pltpu.VMEM((blocks, LANES, LANES), jnp.float32),
-            pltpu.SemaphoreType.DMA((2,)),
+            pltpu.SemaphoreType.DMA((blocks,)),
+            pltpu.SemaphoreType.DMA((blocks,)),
             pltpu.SemaphoreType.DMA,
             pltpu.SemaphoreType.DMA,
             pltpu.SemaphoreType.DMA((count,)),

time: 170 us -> 166 us (0.976)
  Pallas kernels: 164 us -> 159 us
    pallas_call x1, Pallas kernels: 164 us -> 159 us  [local(): pl.pallas_call(kernel, out_shape=jax.ShapeDtypeStruct((rows, width), jnp....]
where the time goes in v6:
time: 166 us; the launch traced here: 165 us
  Pallas kernels  159 us (96%)
  local copies, waits for them, and re-layouts  5.31 us (3%)
    pallas_call x1, Pallas kernels, local(): pl.pallas_call(kernel, out_shape=jax.ShapeDtypeStruct((rows, width), jnp....  159 us
    unnamed x2, local copies, waits for them, and re-layouts  3.87 us

profile of v6, /device:TPU:20, one launch (start us, length us, event | category | flops | bytes accessed | tf_op | source)
XLA Modules:
  0.0 165.2 jit_solution(9546642269781157608)
XLA Ops:
  0.0 0.7 sqrt_multiply_fusion
  0.7 0.1 copy.9
  0.8 0.7 reshape.7.weight_ref
  1.5 0.8 copy.8
  2.3 0.7 reshape.6.rate_ref
  2.9 159.2 %shard_map.55 = bf16[128,8192]{1,0:T(8,128)(2,1)} custom-call(bf16[3,1024,1024]{2,1,0:T(8,128)(2,1)} %proj.1, f32[3,3,1024]{2,1,0:T(4,128)} %taps.1, f32[8,128]{1,0:T(8,128)} %reshape.6.rate_ref, f32[8,128]{1,0:T(8,128)} %reshape.7.weight_ref, bf16[1024,8192]{1,0:T(8,128)(2,1)} %w_ref.1), custom_call_target="tpu_custom_call" | custom-call | tf_op jit(solution)/shard_map/pallas_call | solution.py:509
  162.1 3.1 %copy.11 = bf16[128,8192]{1,0:T(8,128)(2,1)} copy(bf16[128,8192]{1,0:T(8,128)(2,1)} %shard_map.55) | data formatting | bytes 4194304
